TPU v7x, 32 devices: a whole 2x2x4 slice. The times are simulated.
32 devices in a mesh: section: 2 (over y), grp: 4 (over z), shard: 4 (over x, core).
Axes of the slice: x: 2, y: 2, z: 4, core: 2. Of those that a mesh axis runs over, the one named last changes fastest.
Arguments:
- start: bfloat16 [32, 256, 1152], P(('grp', 'shard')), may hold values from -6 to 6
- out_grad: bfloat16 [32, 256, 1152], P(('grp', 'shard')), may hold values from -6 to 6
- extra_images: int32 [16], P(('grp', 'shard')), may hold values from 0 to 1
- timesteps: int32 [32], P(('grp', 'shard')), may hold values from 0 to 999
- labels: int32 [32], P(('grp', 'shard')), may hold values from 0 to 999
- embed_table: float32 [2000, 1152], P(None, 'section'), may hold values from -6 to 6
- w_qkv: float32 [2, 1152, 3456], P('section', 'shard'), may hold values from -0.1875 to 0.1875
- w_out: float32 [2, 1152, 1152], P('section', 'shard'), may hold values from -0.75 to 0.75
- w_gu: float32 [2, 1152, 6144], P('section', 'shard'), may hold values from -0.1875 to 0.1875
- w_ada: float32 [2, 1152, 6912], P('section', 'shard'), may hold values from -0.1875 to 0.1875
- w_down: float32 [2, 3072, 1152], P('section', None, 'shard'), may hold values from -0.109375 to 0.109375
- small_params: float32 [2, 11664], P('section', 'shard'), may hold values from -0.35 to 1.25, as said below
- feature_moments: float32 [2, 5, 1152], P('section', None, 'shard'), may hold values from 409 to 8192
- other_moments: float32 [2, 20736], P('section'), may hold values from 409 to 8192
- small_moment: float32 [2, 11664], P('section', 'shard'), may hold values from 819 to 32768
Outputs:
- section_out: bfloat16 [2, 32, 256, 1152], P('section', ('grp', 'shard'))
- section_in_grad: bfloat16 [2, 32, 256, 1152], P('section', ('grp', 'shard'))
- cond_grad: float32 [32, 1152], P(('grp', 'shard'), 'section')
- grad_qkv: float32 [2, 1152, 3456], P('section', 'shard')
- grad_out: float32 [2, 1152, 1152], P('section', 'shard')
- grad_gu: float32 [2, 1152, 6144], P('section', 'shard')
- grad_ada: float32 [2, 1152, 6912], P('section', 'shard')
- grad_down: float32 [2, 3072, 1152], P('section', None, 'shard')
- grad_small: float32 [2, 11664], P('section', 'shard')
- new_qkv: float32 [2, 1152, 3456], P('section', 'shard')
- new_out: float32 [2, 1152, 1152], P('section', 'shard')
- new_gu: float32 [2, 1152, 6144], P('section', 'shard')
- new_ada: float32 [2, 1152, 6912], P('section', 'shard')
- new_down: float32 [2, 3072, 1152], P('section', None, 'shard')
- new_small: float32 [2, 11664], P('section', 'shard')
- new_feature_moments: float32 [2, 5, 1152], P('section', None, 'shard')
- new_other_moments: float32 [2, 20736], P('section')
- new_small_moment: float32 [2, 11664], P('section', 'shard')
Inputs may be any that keep to these rules, and one draw needn't show every extreme that they name: A device's first extra_images + 1 micro-batches hold live images, the rest padding. `small_params`: biases lie within 0.35 of zero, gains between 0.75 and 1.25.
All inputs are finite; a program needn't handle non-finite values.
Results may differ from a plain program's by a relative error of at most 0.024.
Values may be sent and summed in bfloat16 or wider, within the bound.
A program may use at most 384 MiB of HBM per device.

v0:
```python
import functools

import jax
import jax.numpy as jnp
import numpy as np
from jax import lax
from jax.experimental import pallas as pl
from jax.experimental.pallas import tpu as pltpu
from jax.sharding import PartitionSpec as P

HEADS = 16
FF = 3072
GRID = 16
MB = 2
TIMESTEPS = 1000
HEAD_DIM = 72
LEN = 256


EPS = 1e-06
TINY = 1e-30
RATE = 0.04
RATE_SMALL = 0.05
DECAY = 0.5
CHUNK = 384
AHEAD = 3
LAG = 2
SLOTS = 6
HOP = 2
MESH = pl.DeviceIdType.MESH
RING = 10
ROWS = 32
NT = (((1,), (1,)), ((), ()))
TN = (((0,), (0,)), ((), ()))
PAD = 128


def passed_along(block, axis, distance):
    devices = range(lax.axis_size(axis))
    route = [(i - distance, i) for i in devices if i - distance in devices]
    return lax.ppermute(block, axis, route)


def rope_tables(model_width):
    quarter = HEAD_DIM // 4
    tokens = np.arange(LEN)
    inverse = np.float32(10000.0) ** (-np.arange(quarter).astype(np.float32) / quarter)
    row_angle = (tokens // GRID).astype(np.float32)[:, None] * inverse[None, :]
    col_angle = (tokens % GRID).astype(np.float32)[:, None] * inverse[None, :]
    angles = np.concatenate([row_angle, row_angle, col_angle, col_angle], axis=1)
    lane = np.arange(HEAD_DIM) % (HEAD_DIM // 2)
    sines = np.sin(angles)
    first = np.where(lane < quarter, -sines, 0.0)
    second = np.where(lane >= quarter, sines, 0.0)
    count = model_width // HEAD_DIM
    return tuple(
        jnp.asarray(np.tile(table, (1, count)), jnp.float32)
        for table in (np.cos(angles), first, second)
    )


def head_members(model_width):
    owner = np.arange(model_width)[:, None] // HEAD_DIM
    return jnp.asarray(owner == np.arange(PAD)[None, :], jnp.bfloat16)


def dot_back(incoming, matrix):
    return mul(incoming, matrix, NT)


def place():
    return lax.axis_index("section"), lax.axis_index("grp"), lax.axis_index("shard")


def gather_kernel(chips, own_ref, all_ref, here_sem, sib_sem, x_sem, z_sem, f_sem):
    sec, grp, me = place()
    core = me % 2
    chip = me // 2
    half = grp % 2
    count = own_ref.shape[0] // 2
    sibling = (sec, grp, me ^ 1)
    across = (sec, grp ^ 1, me)

    barrier = pltpu.get_barrier_semaphore()
    pl.semaphore_signal(barrier, inc=1, device_id=sibling, device_id_type=MESH)
    pl.semaphore_signal(barrier, inc=1, device_id=across, device_id_type=MESH)
    for k in range(1, chips):
        pl.semaphore_signal(
            barrier, inc=1, device_id=(sec, grp, 2 * (chip ^ k) + core), device_id_type=MESH
        )
    pl.semaphore_wait(barrier, chips + 1)

    def chip_copy(k, step):
        piece = 2 * step + half
        return pltpu.make_async_remote_copy(
            src_ref=own_ref.at[piece],
            dst_ref=all_ref.at[piece, me],
            send_sem=x_sem.at[0, k - 1, step],
            recv_sem=x_sem.at[1, k - 1, step],
            device_id=(sec, grp, 2 * (chip ^ k) + core),
            device_id_type=MESH,
        )

    def chip_arrival(k, step):
        piece = 2 * step + half
        owner = 2 * (chip ^ k) + core
        return pltpu.make_async_remote_copy(
            src_ref=own_ref.at[piece],
            dst_ref=all_ref.at[piece, owner],
            send_sem=x_sem.at[0, k - 1, step],
            recv_sem=x_sem.at[1, k - 1, step],
            device_id=(sec, grp, owner),
            device_id_type=MESH,
        )

    def onward(k, step, side, sems, row, target):
        owner = 2 * (chip ^ k) + core
        region = all_ref.at[2 * step + side, owner]
        return pltpu.make_async_remote_copy(
            src_ref=region,
            dst_ref=region,
            send_sem=sems.at[0, row, step],
            recv_sem=sems.at[1, row, step],
            device_id=target,
            device_id_type=MESH,
        )

    def from_sibling(k, step, side, row):
        owner = 2 * (chip ^ k) + 1 - core
        region = all_ref.at[2 * step + side, owner]
        return pltpu.make_async_remote_copy(
            src_ref=region,
            dst_ref=region,
            send_sem=f_sem.at[0, row, step],
            recv_sem=f_sem.at[1, row, step],
            device_id=sibling,
            device_id_type=MESH,
        )

    def beside(step):
        pair = pl.ds(2 * step, 2)
        return pltpu.make_async_remote_copy(
            src_ref=own_ref.at[pair],
            dst_ref=all_ref.at[pair, me],
            send_sem=sib_sem.at[0, step],
            recv_sem=sib_sem.at[1, step],
            device_id=sibling,
            device_id_type=MESH,
        )

    def start_chip(step):
        for k in range(1, chips):
            chip_copy(k, step).start()

    for step in range(AHEAD):
        start_chip(step)
    here = pltpu.make_async_copy(own_ref, all_ref.at[:, me], here_sem)
    here.start()

    def relay(step, carry):
        @pl.when(step < count)
        def _():
            for k in range(1, chips):
                chip_arrival(k, step).wait_recv()
                onward(k, step, half, z_sem, k - 1, across).start()
                onward(k, step, half, f_sem, 2 * (k - 1), sibling).start()
                chip_copy(k, step).wait_send()
            beside(step).start()

        @pl.when(step + AHEAD < count)
        def _():
            start_chip(step + AHEAD)

        @pl.when(step >= LAG)
        def _():
            for k in range(1, chips):
                onward(k, step - LAG, 1 - half, z_sem, k - 1, across).wait_recv()
                onward(k, step - LAG, 1 - half, f_sem, 2 * (k - 1) + 1, sibling).start()
                onward(k, step - LAG, half, z_sem, k - 1, across).wait_send()

        return carry

    lax.fori_loop(0, count + LAG, relay, 0)

    def finish(step, carry):
        for k in range(1, chips):
            onward(k, step, half, f_sem, 2 * (k - 1), sibling).wait_send()
            onward(k, step, 1 - half, f_sem, 2 * (k - 1) + 1, sibling).wait_send()
            from_sibling(k, step, half, 2 * (k - 1)).wait_recv()
            from_sibling(k, step, 1 - half, 2 * (k - 1) + 1).wait_recv()
        beside(step).wait()
        return carry

    lax.fori_loop(0, count, finish, 0)
    here.wait()


def gather_rows(own):
    shards = lax.axis_size("shard")
    chips = shards // 2
    chunks, rows, width = own.shape
    count = chunks // 2
    return pl.pallas_call(
        functools.partial(gather_kernel, chips),
        out_shape=jax.ShapeDtypeStruct((chunks, shards, rows, width), own.dtype),
        in_specs=[pl.BlockSpec(memory_space=pltpu.VMEM)],
        out_specs=pl.BlockSpec(memory_space=pl.ANY),
        scratch_shapes=[
            pltpu.SemaphoreType.DMA,
            pltpu.SemaphoreType.DMA((2, count)),
            pltpu.SemaphoreType.DMA((2, chips - 1, count)),
            pltpu.SemaphoreType.DMA((2, chips - 1, count)),
            pltpu.SemaphoreType.DMA((2, 2 * (chips - 1), count)),
        ],
        compiler_params=pltpu.CompilerParams(
            collective_id=0, has_side_effects=True, vmem_limit_bytes=32 * 1024 * 1024
        ),
        cost_estimate=pl.CostEstimate(flops=0, bytes_accessed=300_000_000, transcendentals=0),
        name="gather_rows",
    )(own)


def reduce_kernel(shards, groups, firsts, pieces, *refs):
    matrices = len(firsts)
    left_refs, refs = refs[:MB], refs[MB:]
    right_refs, refs = refs[: MB * matrices], refs[MB * matrices :]
    pack_ref, act_ref, ada_ref, tail_ref, refs = *refs[:4], refs[4:]
    sum_refs, refs = refs[:matrices], refs[matrices:]
    (
        rowsq_ref,
        stats_ref,
        total_ref,
        mods_ref,
        acts_ref,
        cond_ref,
        right_buf,
        send1,
        keep1,
        recv1,
        send2,
        recv2,
        keep2,
        keep3,
        send3,
        recv3,
        final,
        recv5,
        spread,
        mods,
        part,
        part_in,
        stats,
        stats_in,
        stats_all,
        right_sem,
        sem1,
        sem2,
        sem3,
        sem5,
        out_sem,
        chip_sem,
        line_sem,
        swap_sem,
        cond_sem,
        stat_sem,
    ) = refs
    chips = shards // 2
    ends = 2 * groups
    rows = rowsq_ref.shape[1]
    bounds = list(firsts) + [sum(ref.shape[1] for ref in sum_refs) // CHUNK]
    total = bounds[-1]
    model_width = mods.shape[2]
    per_group = acts_ref.shape[1]
    low, high = jnp.bfloat16, jnp.float32
    sec, grp, me = place()
    core = me % 2
    chip = me // 2
    middle = groups // 2
    lower = grp < middle
    depth = jnp.where(lower, middle - 1 - grp, grp - middle)
    inner = jnp.where(lower, grp + 1, grp - 1)
    outer = jnp.where(lower, grp - 1, grp + 1)
    has_outer = depth < middle - 1
    sibling = (sec, grp, me ^ 1)
    across = (1 - sec, grp, me)

    def chip_peer(k):
        return (sec, grp, 2 * (chip ^ k) + core)

    barrier = pltpu.get_barrier_semaphore()
    pl.semaphore_signal(barrier, inc=1, device_id=sibling, device_id_type=MESH)
    pl.semaphore_signal(barrier, inc=1, device_id=across, device_id_type=MESH)
    for k in range(1, chips):
        pl.semaphore_signal(barrier, inc=1, device_id=chip_peer(k), device_id_type=MESH)
    pl.semaphore_signal(barrier, inc=1, device_id=(sec, inner, me), device_id_type=MESH)

    @pl.when(has_outer)
    def _():
        pl.semaphore_signal(barrier, inc=1, device_id=(sec, outer, me), device_id_type=MESH)

    pl.semaphore_wait(barrier, chips + 2 + jnp.where(has_outer, 1, 0))

    def which(item):
        matrix = 0
        for first in firsts[1:]:
            matrix = matrix + jnp.where(item >= first, 1, 0)
        return matrix

    def in_matrix(item, matrix):
        return (item >= bounds[matrix]) & (item < bounds[matrix + 1])

    def columns(item, matrix):
        return pl.ds(pl.multiple_of((item - firsts[matrix]) * CHUNK, CHUNK), CHUNK)

    def fetch(item):
        slot = item % 3
        for matrix in range(matrices):

            @pl.when(in_matrix(item, matrix))
            def _():
                for micro in range(MB):
                    pltpu.make_async_copy(
                        right_refs[micro * matrices + matrix].at[:, columns(item, matrix)],
                        right_buf.at[slot, micro],
                        right_sem.at[slot, micro],
                    ).start()

    def arrived(item):
        for micro in range(MB):
            slot = item % 3
            pltpu.make_async_copy(
                right_refs[0].at[:, pl.ds(0, CHUNK)],
                right_buf.at[slot, micro],
                right_sem.at[slot, micro],
            ).wait()

    def remote(source, target, sems, device):
        return pltpu.make_async_remote_copy(
            src_ref=source,
            dst_ref=target,
            send_sem=sems[0],
            recv_sem=sems[1],
            device_id=device,
            device_id_type=MESH,
        )

    def copy1(item):
        slot = item % SLOTS
        sems = (sem1.at[0, slot], sem1.at[1, slot])
        return remote(send1.at[slot], recv1.at[slot], sems, sibling)

    def copy2(item, k):
        slot = item % SLOTS
        sems = (sem2.at[0, slot, k - 1], sem2.at[1, slot, k - 1])
        return remote(send2.at[slot, k - 1], recv2.at[slot, k - 1], sems, chip_peer(k))

    def copy3(item, kind):
        slot = item % SLOTS
        sems = (sem3.at[0, 0, slot], sem3.at[1, kind, slot])
        return remote(send3.at[slot], recv3.at[kind, slot], sems, (sec, inner, me))

    def copy5(item):
        slot = item % ends
        sems = (sem5.at[0, slot], sem5.at[1, slot])
        return remote(final.at[slot], recv5.at[slot], sems, (sec, outer, me))

    def start_out(item):
        slot = item % ends
        for matrix in range(matrices):

            @pl.when(in_matrix(item, matrix))
            def _():
                pltpu.make_async_copy(
                    final.at[slot], sum_refs[matrix].at[:, columns(item, matrix)], out_sem.at[slot]
                ).start()

    def wait_out(item):
        slot = item % ends
        pltpu.make_async_copy(
            final.at[slot], sum_refs[0].at[:, pl.ds(0, CHUNK)], out_sem.at[slot]
        ).wait()

    def chip_spread(k, owner):
        region = spread.at[core, grp, owner]
        sems = (chip_sem.at[0, k - 1], chip_sem.at[1, k - 1])
        return remote(region, region, sems, chip_peer(k))

    def line_spread(side, step, row):
        target = (sec, grp + 1 - 2 * side, me)
        region = spread.at[core, row]
        second = acts_ref.at[row]
        return (
            remote(
                region, region, (line_sem.at[0, side, step, 0], line_sem.at[1, side, step, 0]), target
            ),
            remote(
                second, second, (line_sem.at[0, side, step, 1], line_sem.at[1, side, step, 1]), target
            ),
        )

    def swap_spread(which_core):
        region = spread.at[which_core]
        return remote(region, region, (swap_sem.at[0], swap_sem.at[1]), sibling)

    def cond_across():
        return remote(part, part_in, (cond_sem.at[0, 0], cond_sem.at[1, 0]), across)

    def cond_beside(owner):
        region = cond_ref.at[owner]
        return remote(region, region, (cond_sem.at[0, 1], cond_sem.at[1, 1]), sibling)

    def cond_chip(k, owner):
        region = cond_ref.at[pl.ds(2 * owner, 2)]
        sems = (cond_sem.at[0, 1 + k], cond_sem.at[1, 1 + k])
        return remote(region, region, sems, chip_peer(k))

    def exists(side):
        return (grp < groups - 1) if side == 0 else (grp > 0)

    swap_tick = 2 + 2 * groups
    piece_tick = swap_tick + 2
    cond_tick = piece_tick + pieces

    def beside_the_sum(tick):
        @pl.when(tick == 2)
        def _():
            for k in range(1, chips):
                chip_spread(k, chip ^ k).wait_recv()
            for side in range(2):

                @pl.when(exists(side))
                def _():
                    for copy in line_spread(side, 0, grp):
                        copy.start()

        for step in range(1, groups):

            @pl.when(tick == 2 + 2 * step)
            def _():
                for side in range(2):
                    row = grp - step if side == 0 else grp + step
                    came = (row >= 0) if side == 0 else (row < groups)

                    @pl.when(came)
                    def _():
                        for copy in line_spread(side, step - 1, row):
                            copy.wait_recv()

                    @pl.when(came & exists(side))
                    def _():
                        for copy in line_spread(side, step, row):
                            copy.start()

        @pl.when(tick == swap_tick)
        def _():
            swap_spread(core).start()

        @pl.when(tick == piece_tick)
        def _():
            swap_spread(1 - core).wait_recv()
            mods[...] = jnp.zeros_like(mods)
            total_ref[...] = jnp.zeros_like(total_ref)

            def unpack(index, carry):
                origin = index // (groups * chips)
                row = (index // chips) % groups
                owner = index % chips
                block = spread[origin, row, owner].astype(high)
                total_ref[...] = total_ref[...] + block
                first = row * per_group + (2 * owner + origin) * MB
                for micro in range(MB):
                    for piece in range(pieces):
                        line = micro * pieces + piece
                        mods[piece, pl.ds(first + micro, 1), :] = block[
                            line : line + 1, :model_width
                        ]
                return carry

            lax.fori_loop(0, 2 * groups * chips, unpack, 0)
            part[...] = jnp.zeros_like(part)
            rowsq_ref[matrices] = jnp.zeros_like(rowsq_ref[matrices])

        for piece in range(pieces):

            @pl.when(tick == piece_tick + piece)
            def _():
                every = acts_ref[...].reshape(groups * per_group, acts_ref.shape[2])
                mod = mods[piece].astype(low)
                mods_ref[piece] = mod
                value = mul(every, mod, TN)[:rows]
                square = value * value + TINY
                folded = square[:, :128]
                for start in range(128, model_width, 128):
                    folded = folded + square[:, start : start + 128]
                rowsq_ref[matrices] = rowsq_ref[matrices] + folded
                sums = jnp.sum(square, axis=0, keepdims=True)
                split = model_width // CHUNK
                for index in range(split):
                    line = total + piece * split + index
                    stats[line : line + 1] = sums[:, index * CHUNK : (index + 1) * CHUNK]
                mine = mods[piece, pl.ds(pl.multiple_of(grp * per_group, 8), per_group), :]
                back = mul(
                    mine.astype(low), ada_ref[:, piece * model_width : (piece + 1) * model_width], NT
                )
                part[:, :rows] = part[:, :rows] + back

        @pl.when(tick == cond_tick)
        def _():
            cond_across().start()

        @pl.when(tick == cond_tick + 2)
        def _():
            cond_across().wait_recv()
            cond_ref[me] = part[...] + part_in[...]
            cond_beside(me).start()

        @pl.when(tick == cond_tick + 4)
        def _():
            cond_beside(me ^ 1).wait_recv()
            for k in range(1, chips):
                cond_chip(k, chip).start()

        @pl.when(tick == cond_tick + 6)
        def _():
            for k in range(1, chips):
                cond_chip(k, chip ^ k).wait_recv()

    def beside_the_sum_sent():
        for k in range(1, chips):
            chip_spread(k, chip).wait_send()
            cond_chip(k, chip).wait_send()
        for side in range(2):
            for step in range(groups - 1):
                row = grp - step if side == 0 else grp + step
                came = (row >= 0) if side == 0 else (row < groups)

                @pl.when(came & exists(side))
                def _():
                    for copy in line_spread(side, step, row):
                        copy.wait_send()

        swap_spread(core).wait_send()
        cond_across().wait_send()
        cond_beside(me).wait_send()

    send_kind = jnp.where(depth == 0, 1, 0)
    lag3 = 1 + HOP * (middle - depth)
    lag5 = 1 + HOP * (middle + 1 + depth)
    held = HOP * (middle - 1) + 1
    rowsq_ref[...] = jnp.zeros_like(rowsq_ref)
    stats[...] = jnp.zeros_like(stats)
    stats[stats.shape[0] - 1 :] = tail_ref[...]
    spread[core, grp, chip] = pack_ref[...]
    acts_ref[grp] = act_ref[...]
    for k in range(1, chips):
        chip_spread(k, chip).start()
    fetch(0)
    fetch(1)

    def step(tick, carry):
        item0 = tick

        @pl.when(item0 < total)
        def _():
            slot = item0 % SLOTS

            @pl.when(item0 >= SLOTS)
            def _():
                copy1(item0 - SLOTS).wait_send()

            @pl.when(item0 + 2 < total)
            def _():
                fetch(item0 + 2)

            arrived(item0)
            matrix = which(item0)

            def product(shard):
                value = 0.0
                for micro in range(MB):
                    value = value + jnp.dot(
                        left_refs[micro][matrix, shard],
                        right_buf[item0 % 3, micro],
                        preferred_element_type=high,
                    )
                return value

            def multiply(k, carry):
                send1[slot, k] = product(2 * k + 1 - core).astype(low)
                keep1[item0 % 2, k] = product(2 * k + core)
                return carry

            lax.fori_loop(0, chips, multiply, 0)
            copy1(item0).start()

        item1 = tick - 1

        @pl.when((item1 >= 0) & (item1 < total))
        def _():
            slot = item1 % SLOTS
            copy1(item1).wait_recv()

            @pl.when(item1 >= SLOTS)
            def _():
                for k in range(1, chips):
                    copy2(item1 - SLOTS, k).wait_send()

            for k in range(1, chips):
                other = chip ^ k
                send2[slot, k - 1] = (
                    keep1[item1 % 2, other] + recv1[slot, other].astype(high)
                ).astype(low)
                copy2(item1, k).start()
            keep2[item1 % (HOP + 1)] = keep1[item1 % 2, chip] + recv1[slot, chip].astype(high)

        item2 = tick - 1 - HOP

        @pl.when((item2 >= 0) & (item2 < total))
        def _():
            slot = item2 % SLOTS
            value = keep2[item2 % (HOP + 1)]
            for k in range(1, chips):
                copy2(item2, k).wait_recv()
                value = value + recv2[slot, k - 1].astype(high)
            keep3[item2 % held] = value

        item3 = tick - lag3

        @pl.when((item3 >= 0) & (item3 < total))
        def _():
            slot = item3 % SLOTS

            @pl.when(item3 >= SLOTS)
            def _():
                copy3(item3 - SLOTS, send_kind).wait_send()

            @pl.when(has_outer)
            def _():
                copy3(item3, 0).wait_recv()
                send3[slot] = (keep3[item3 % held] + recv3[0, slot].astype(high)).astype(low)

            @pl.when(jnp.logical_not(has_outer))
            def _():
                send3[slot] = keep3[item3 % held].astype(low)

            copy3(item3, send_kind).start()

        item5 = tick - lag5

        @pl.when((item5 >= 0) & (item5 < total))
        def _():
            slot = item5 % ends
            other = item5 % SLOTS

            @pl.when(item5 >= ends)
            def _():
                wait_out(item5 - ends)

                @pl.when(has_outer)
                def _():
                    copy5(item5 - ends).wait_send()

            @pl.when(depth == 0)
            def _():
                copy3(item5, 1).wait_recv()
                final[slot] = (send3[other].astype(high) + recv3[1, other].astype(high)).astype(low)

            @pl.when(depth > 0)
            def _():
                copy5(item5).wait_recv()
                final[slot] = recv5[slot]

            @pl.when(has_outer)
            def _():
                copy5(item5).start()

            start_out(item5)
            value = final[slot].astype(high)
            square = value * value + TINY
            folded = square[:, :128]
            for start in range(128, CHUNK, 128):
                folded = folded + square[:, start : start + 128]
            matrix = which(item5)
            rowsq_ref[matrix] = rowsq_ref[matrix] + folded
            stats[pl.ds(item5, 1), :] = jnp.sum(square, axis=0, keepdims=True)

        beside_the_sum(tick)
        return carry

    lax.fori_loop(0, total + 1 + 2 * HOP * middle, step, 0)

    beside = remote(stats, stats_in, (stat_sem.at[0, 0], stat_sem.at[1, 0]), sibling)
    beside.start()
    beside.wait_recv()
    stats_all[chip] = stats[...] + stats_in[...]

    def stat_chip(k, owner):
        region = stats_all.at[owner]
        return remote(region, region, (stat_sem.at[0, k], stat_sem.at[1, k]), chip_peer(k))

    for k in range(1, chips):
        stat_chip(k, chip).start()
    for k in range(1, chips):
        stat_chip(k, chip ^ k).wait_recv()
    value = stats_all[0]
    for owner in range(1, chips):
        value = value + stats_all[owner]
    stats_ref[...] = value

    def drain(offset, carry):
        item = total - SLOTS + offset
        copy1(item).wait_send()
        for k in range(1, chips):
            copy2(item, k).wait_send()
        copy3(item, send_kind).wait_send()
        return carry

    lax.fori_loop(0, SLOTS, drain, 0)

    def drain_out(offset, carry):
        item = total - ends + offset
        wait_out(item)

        @pl.when(has_outer)
        def _():
            copy5(item).wait_send()

        return carry

    lax.fori_loop(0, ends, drain_out, 0)
    beside_the_sum_sent()
    beside.wait_send()
    for k in range(1, chips):
        stat_chip(k, chip).wait_send()


def reduce_grads(lefts, rights, packed, act, ada, tail):
    shards = lax.axis_size("shard")
    groups = lax.axis_size("grp")
    chips = shards // 2
    middle = groups // 2
    ends = 2 * groups
    matrices, _, rows, tokens = lefts[0].shape
    widths = [right.shape[1] for right in rights[0]]
    firsts = [sum(widths[:index]) // CHUNK for index in range(matrices)]
    model_width = shards * rows
    pieces = ada.shape[1] // model_width
    lines = sum(widths) // CHUNK + ada.shape[1] // CHUNK + 1
    low, high = jnp.bfloat16, jnp.float32
    block = (rows, CHUNK)
    near = pl.BlockSpec(memory_space=pltpu.VMEM)
    far = pl.BlockSpec(memory_space=pl.ANY)
    every = groups * act.shape[0]
    return pl.pallas_call(
        functools.partial(reduce_kernel, shards, groups, firsts, pieces),
        out_shape=[jax.ShapeDtypeStruct((rows, width), low) for width in widths]
        + [
            jax.ShapeDtypeStruct((matrices + 1, rows, 128), high),
            jax.ShapeDtypeStruct((lines, CHUNK), high),
            jax.ShapeDtypeStruct(packed.shape, high),
            jax.ShapeDtypeStruct((pieces, every, model_width), low),
            jax.ShapeDtypeStruct((groups,) + act.shape, low),
            jax.ShapeDtypeStruct((shards,) + act.shape, high),
        ],
        in_specs=[near] * MB + [far] * (MB * matrices) + [near] * 4,
        out_specs=[far] * matrices + [near] * 6,
        scratch_shapes=[
            pltpu.VMEM((3, MB, tokens, CHUNK), low),
            pltpu.VMEM((SLOTS, chips) + block, low),
            pltpu.VMEM((2, chips) + block, high),
            pltpu.VMEM((SLOTS, chips) + block, low),
            pltpu.VMEM((SLOTS, chips - 1) + block, low),
            pltpu.VMEM((SLOTS, chips - 1) + block, low),
            pltpu.VMEM((HOP + 1,) + block, high),
            pltpu.VMEM((HOP * (middle - 1) + 1,) + block, high),
            pltpu.VMEM((SLOTS,) + block, low),
            pltpu.VMEM((2, SLOTS) + block, low),
            pltpu.VMEM((ends,) + block, low),
            pltpu.VMEM((ends,) + block, low),
            pltpu.VMEM((2, groups, chips) + packed.shape, low),
            pltpu.VMEM((pieces, every, model_width), high),
            pltpu.VMEM(act.shape, high),
            pltpu.VMEM(act.shape, high),
            pltpu.VMEM((lines, CHUNK), high),
            pltpu.VMEM((lines, CHUNK), high),
            pltpu.VMEM((chips, lines, CHUNK), high),
            pltpu.SemaphoreType.DMA((3, MB)),
            pltpu.SemaphoreType.DMA((2, SLOTS)),
            pltpu.SemaphoreType.DMA((2, SLOTS, chips - 1)),
            pltpu.SemaphoreType.DMA((2, 2, SLOTS)),
            pltpu.SemaphoreType.DMA((2, ends)),
            pltpu.SemaphoreType.DMA((ends,)),
            pltpu.SemaphoreType.DMA((2, chips - 1)),
            pltpu.SemaphoreType.DMA((2, 2, groups, 2)),
            pltpu.SemaphoreType.DMA((2,)),
            pltpu.SemaphoreType.DMA((2, chips + 1)),
            pltpu.SemaphoreType.DMA((2, chips)),
        ],
        compiler_params=pltpu.CompilerParams(
            collective_id=1, has_side_effects=True, vmem_limit_bytes=56 * 1024 * 1024
        ),
        cost_estimate=pl.CostEstimate(flops=0, bytes_accessed=600_000_000, transcendentals=0),
        name="reduce_grads",
    )(*lefts, *[right for group in rights for right in group], packed, act, ada, tail)


def mul(left, right, form=(((1,), (0,)), ((), ()))):
    return lax.dot_general(left, right, form, preferred_element_type=jnp.float32)


def halves(value):
    upper = value.astype(jnp.bfloat16)
    return upper, (value - upper.astype(jnp.float32)).astype(jnp.bfloat16)


def mul_split(value, right, form=(((1,), (0,)), ((), ()))):
    upper, lower = halves(value)
    return mul(upper, right, form) + mul(lower, right, form)


def by_rows(work, init=0, size=ROWS):
    def step(index, carry):
        return work(pl.ds(pl.multiple_of(index * size, size), size), carry)

    return lax.fori_loop(0, LEN // size, step, init)


def aligned(start, size):
    return pl.ds(pl.multiple_of(start, 128), size)


def rms_rate(value):
    return lax.rsqrt(jnp.mean(value * value, axis=-1, keepdims=True) + EPS)


def turn(value, cosines, first, second):
    width = value.shape[1]
    quarter = HEAD_DIM // 4
    ahead = pltpu.roll(value, width - quarter, 1)
    behind = pltpu.roll(value, quarter, 1)
    return value * cosines, ahead * first + behind * second


def window(head, model_width):
    tile = jnp.minimum(head * HEAD_DIM // 128, model_width // 128 - 2)
    lane = lax.broadcasted_iota(jnp.int32, (1, 256), 1) + tile * 128 - head * HEAD_DIM
    mask = ((lane >= 0) & (lane < HEAD_DIM)).astype(jnp.bfloat16)
    return aligned(tile * 128, 256), mask


def ring_of(weights, ring, sems, order, count):
    def copy(item):
        slot = item % RING
        return pltpu.make_async_copy(weights.at[order(item)], ring.at[slot], sems.at[slot])

    def begin():
        for item in range(RING):
            copy(item).start()

    def ready(item):
        copy(item).wait()
        return item % RING

    def release(item):
        @pl.when(item + RING < count)
        def _():
            copy(item + RING).start()

    return begin, ready, release


def forward_kernel(
    active,
    live,
    x_ref,
    weights,
    mod_ref,
    bias_ref,
    gain_ref,
    cos_ref,
    first_ref,
    second_ref,
    member_ref,
    *rest,
    aliased,
):
    rest = rest[aliased:]
    out_ref, leave_ref, left_out, hid_out, low_out, prob_out, high_out, gu_out = rest[:8]
    (
        ring,
        a_buf,
        qkv,
        low_buf,
        prob,
        high_buf,
        gu_buf,
        hid,
        left,
        acc,
        out_buf,
        leave_buf,
        ring_sem,
        out_sem,
    ) = rest[8:]
    model_width = x_ref.shape[1]
    low, high = jnp.bfloat16, jnp.float32
    heads = model_width // HEAD_DIM
    chunks = weights.shape[0]
    wide = CHUNK

    @pl.when(active[0] == 1)
    def _():
        begin, ready, release = ring_of(weights, ring, ring_sem, lambda item: item, chunks)
        begin()
        copies = []

        def send(source, target):
            copy = pltpu.make_async_copy(source, target, out_sem.at[len(copies)])
            copy.start()
            copies.append(copy)

        shift1, scale1, gate1 = mod_ref[0:1], mod_ref[1:2], mod_ref[2:3]
        shift2, scale2, gate2 = mod_ref[3:4], mod_ref[4:5], mod_ref[5:6]

        def enter(rows, carry):
            x = x_ref[rows].astype(high)
            a_buf[rows] = (x * rms_rate(x) * (1.0 + scale1) + shift1).astype(low)
            return carry

        by_rows(enter)

        def project(item, carry):
            slot = ready(item)
            cols = aligned(item * wide, wide)
            qkv[:, cols] = mul(a_buf[...], ring[slot]) + bias_ref[:, cols]
            release(item)
            return carry

        qkv_chunks = 3 * model_width // wide
        lax.fori_loop(0, qkv_chunks, project, 0)
        left[0] = a_buf[...].T
        send(left.at[0], left_out.at[0])

        member = member_ref[...]
        for index in range(2):
            base = index * model_width
            cols = slice(base, base + model_width)
            raw = qkv[:, cols]
            rate = lax.rsqrt(mul_split(raw * raw, member) * (1.0 / HEAD_DIM) + EPS)
            acc[...] = mul_split(rate, member, NT)

            def turned(rows, carry):
                unit = qkv[rows, cols] * acc[rows]
                high_buf[rows, cols] = unit
                gained = unit * gain_ref[index : index + 1]
                straight, crossed = turn(gained, cos_ref[rows], first_ref[rows], second_ref[rows])
                low_buf[rows, cols] = (straight + crossed).astype(low)
                return carry

            by_rows(turned)
            high_buf[:, 5 * model_width + index * PAD : 5 * model_width + (index + 1) * PAD] = rate

        low_buf[:, 2 * model_width :] = qkv[:, 2 * model_width :].astype(low)
        send(low_buf, low_out)
        acc[...] = jnp.zeros_like(acc)

        def attend(head, carry):
            cols, mask = window(head, model_width)
            tile = cols.start
            q = low_buf[:, cols] * mask
            k = low_buf[:, aligned(model_width + tile, 256)]
            v = low_buf[:, aligned(2 * model_width + tile, 256)] * mask
            scores = mul(k, q, NT) * HEAD_DIM ** (-0.5)
            weight = jnp.exp(scores - jnp.max(scores, axis=0, keepdims=True))
            share = (weight * (1.0 / jnp.sum(weight, axis=0, keepdims=True))).astype(low)
            prob[head] = share
            acc[:, cols] = acc[:, cols] + mul(share, v, TN)
            return carry

        lax.fori_loop(0, heads, attend, 0, unroll=2)
        send(prob, prob_out)
        a_buf[...] = acc[...].astype(low)
        left[1] = a_buf[...].T
        send(left.at[1], left_out.at[1])

        out_chunks = model_width // wide

        def mix(index, carry):
            item = qkv_chunks + index
            slot = ready(item)
            cols = aligned(index * wide, wide)
            acc[:, cols] = mul(a_buf[...], ring[slot]) + bias_ref[
                :, aligned(3 * model_width + index * wide, wide)
            ]
            release(item)
            return carry

        lax.fori_loop(0, out_chunks, mix, 0)

        proj_cols = slice(2 * model_width, 3 * model_width)
        middle_cols = slice(3 * model_width, 4 * model_width)
        ffn_cols = slice(4 * model_width, 5 * model_width)

        def between(rows, carry):
            proj = acc[rows]
            high_buf[rows, proj_cols] = proj
            middle = x_ref[rows].astype(high) + gate1 * proj
            high_buf[rows, middle_cols] = middle
            a_buf[rows] = (middle * rms_rate(middle) * (1.0 + scale2) + shift2).astype(low)
            return carry

        by_rows(between)
        left[2] = a_buf[...].T
        send(left.at[2], left_out.at[2])

        gate_chunks = FF // wide

        def widen(index, carry):
            item = qkv_chunks + out_chunks + 2 * index
            cols = aligned(index * wide, wide)
            slot = ready(item)
            gate = mul(a_buf[...], ring[slot])
            release(item)
            slot = ready(item + 1)
            up = mul(a_buf[...], ring[slot])
            release(item + 1)
            gu_buf[:, cols] = gate
            gu_buf[:, aligned(FF + index * wide, wide)] = up
            hid[:, cols] = (gate * (1.0 / (1.0 + jnp.exp(-gate))) * up).astype(low)
            return carry

        lax.fori_loop(0, gate_chunks, widen, 0)
        send(gu_buf, gu_out)
        send(hid, hid_out)
        acc[...] = jnp.zeros_like(acc)

        def narrow(index, carry):
            item = qkv_chunks + out_chunks + 2 * gate_chunks + index
            slot = ready(item)
            acc[...] += mul(hid[:, aligned(index * wide, wide)], ring[slot], NT)
            release(item)
            return carry

        lax.fori_loop(0, gate_chunks, narrow, 0)

        def leave(rows, carry):
            ffn = acc[rows]
            high_buf[rows, ffn_cols] = ffn
            result = high_buf[rows, middle_cols] + gate2 * ffn
            leave_buf[rows] = result.astype(low)
            out_buf[rows] = (result * live[0]).astype(low)
            return carry

        by_rows(leave)
        send(leave_buf, leave_ref)
        send(out_buf, out_ref)
        send(high_buf, high_out)
        for copy in copies:
            copy.wait()


def layer_shapes(model_width):
    low, high = jnp.bfloat16, jnp.float32
    return [
        ((LEN, model_width), low),
        ((LEN, model_width), low),
        ((4, model_width, LEN), low),
        ((LEN, FF), low),
        ((LEN, 3 * model_width), low),
        ((HEADS, LEN, LEN), low),
        ((LEN, 5 * model_width + 2 * PAD), high),
        ((LEN, 2 * FF), high),
    ]


def run_forward(active, live, x, weights, mod, bias, gain, tables, member, kept):
    model_width = x.shape[1]
    low, high = jnp.bfloat16, jnp.float32
    shapes = layer_shapes(model_width)
    flag = pl.BlockSpec(memory_space=pltpu.SMEM)
    near = pl.BlockSpec(memory_space=pltpu.VMEM)
    far = pl.BlockSpec(memory_space=pl.ANY)
    kept = [] if kept is None else list(kept)
    return pl.pallas_call(
        functools.partial(forward_kernel, aliased=len(kept)),
        out_shape=[jax.ShapeDtypeStruct(shape, kind) for shape, kind in shapes],
        in_specs=[flag, flag, near, far] + [near] * 7 + [far] * len(kept),
        out_specs=[far] * len(shapes),
        input_output_aliases={11 + index: index for index in range(len(kept))},
        scratch_shapes=[
            pltpu.VMEM((RING, model_width, CHUNK), low),
            pltpu.VMEM((LEN, model_width), low),
            pltpu.VMEM((LEN, 3 * model_width), high),
            pltpu.VMEM((LEN, 3 * model_width), low),
            pltpu.VMEM((HEADS, LEN, LEN), low),
            pltpu.VMEM((LEN, 5 * model_width + 2 * PAD), high),
            pltpu.VMEM((LEN, 2 * FF), high),
            pltpu.VMEM((LEN, FF), low),
            pltpu.VMEM((3, model_width, LEN), low),
            pltpu.VMEM((LEN, model_width), high),
            pltpu.VMEM((LEN, model_width), low),
            pltpu.VMEM((LEN, model_width), low),
            pltpu.SemaphoreType.DMA((RING,)),
            pltpu.SemaphoreType.DMA((10,)),
        ],
        compiler_params=pltpu.CompilerParams(vmem_limit_bytes=56 * 1024 * 1024),
        cost_estimate=pl.CostEstimate(flops=0, bytes_accessed=80_000_000, transcendentals=0),
        name="layer_forward",
    )(active, live, x, weights, mod, bias, gain, *tables, member, *kept)


def backward_kernel(
    active,
    live,
    dy_ref,
    x_ref,
    weights,
    mod_ref,
    gain_ref,
    cos_ref,
    first_ref,
    second_ref,
    member_ref,
    low_in,
    prob_in,
    high_in,
    gu_in,
    *rest,
    aliased,
):
    rest = rest[aliased:]
    dx_out, left_out, dqkv_out, dproj_out, dgu_out, dmod_out, sums_out = rest[:7]
    (
        ring,
        dy,
        low_buf,
        prob,
        high_buf,
        gu_buf,
        dgu,
        dqkv,
        small,
        left,
        acc,
        middle_grad,
        mixed_grad,
        turned_q,
        turned_k,
        turned_v,
        dmod,
        sums,
        ring_sem,
        in_sem,
        out_sem,
    ) = rest[7:]
    model_width = x_ref.shape[1]
    low, high = jnp.bfloat16, jnp.float32
    heads = model_width // HEAD_DIM
    chunks = weights.shape[0]
    wide = CHUNK
    qkv_chunks = 3 * model_width // wide
    out_chunks = model_width // wide
    gate_chunks = FF // wide
    base = qkv_chunks + out_chunks

    def order(item):
        index = item // 3
        kind = item % 3
        ffn_item = jnp.where(
            kind == 0, base + 2 * gate_chunks + index, base + 2 * index + kind - 1
        )
        late = item - 3 * gate_chunks
        other = jnp.where(late < out_chunks, qkv_chunks + late, late - out_chunks)
        return jnp.where(late < 0, ffn_item, other)

    @pl.when(active[0] == 1)
    def _():
        begin, ready, release = ring_of(weights, ring, ring_sem, order, chunks)
        loads = [
            pltpu.make_async_copy(source, target, in_sem.at[index])
            for index, (source, target) in enumerate(
                ((high_in, high_buf), (gu_in, gu_buf), (low_in, low_buf), (prob_in, prob))
            )
        ]
        loads[0].start()
        loads[1].start()
        begin()
        loads[2].start()
        loads[3].start()
        copies = []

        def send(source, target):
            copy = pltpu.make_async_copy(source, target, out_sem.at[len(copies)])
            copy.start()
            copies.append(copy)

        scale1, gate1 = mod_ref[1:2], mod_ref[2:3]
        scale2, gate2 = mod_ref[4:5], mod_ref[5:6]
        proj_cols = slice(2 * model_width, 3 * model_width)
        middle_cols = slice(3 * model_width, 4 * model_width)
        ffn_cols = slice(4 * model_width, 5 * model_width)
        nothing = jnp.zeros((1, model_width), high)

        def total(value):
            return jnp.sum(value, axis=0, keepdims=True)

        loads[0].wait()

        def enter(rows, gate_sum):
            incoming = dy_ref[rows].astype(high) * live[0]
            dy[rows] = incoming
            small[rows] = (gate2 * incoming).astype(low)
            return gate_sum + total(incoming * high_buf[rows, ffn_cols])

        dmod[5:6] = by_rows(enter, nothing)
        left[...] = small[...].T
        send(left, left_out.at[3])
        acc[...] = jnp.zeros_like(acc)
        loads[1].wait()

        def ffn_back(index, carry):
            item = 3 * index
            slot = ready(item)
            d_hid = mul(small[...], ring[slot])
            release(item)
            cols = aligned(index * wide, wide)
            cols_up = aligned(FF + index * wide, wide)
            gate = gu_buf[:, cols]
            sigma = 1.0 / (1.0 + jnp.exp(-gate))
            gated = gate * sigma
            d_gate = (d_hid * gu_buf[:, cols_up] * (sigma + gated * (1.0 - sigma))).astype(low)
            d_up = (d_hid * gated).astype(low)
            dgu[:, cols] = d_gate
            dgu[:, cols_up] = d_up
            slot = ready(item + 1)
            part = mul(d_gate, ring[slot], NT)
            release(item + 1)
            slot = ready(item + 2)
            acc[...] += part + mul(d_up, ring[slot], NT)
            release(item + 2)
            return carry

        lax.fori_loop(0, gate_chunks, ffn_back, 0)
        send(dgu, dgu_out)

        def between(rows, carry):
            scale_sum, shift_sum, gate_sum = carry
            middle = high_buf[rows, middle_cols]
            rate = rms_rate(middle)
            unit = middle * rate
            back = acc[rows]
            d_unit = back * (1.0 + scale2)
            grad = dy[rows] + rate * (
                d_unit - unit * jnp.mean(d_unit * unit, axis=-1, keepdims=True)
            )
            middle_grad[rows] = grad
            d_proj = (gate1 * grad).astype(low)
            small[rows] = d_proj
            return (
                scale_sum + total(back * unit),
                shift_sum + total(back),
                gate_sum + total(grad * high_buf[rows, proj_cols]),
            )

        scale_sum, shift_sum, gate_sum = by_rows(between, (nothing,) * 3)
        dmod[4:5] = scale_sum
        dmod[3:4] = shift_sum
        dmod[2:3] = gate_sum
        send(small, dproj_out)

        def proj_sum(rows, carry):
            return carry + total(small[rows].astype(high))

        sums[3:4] = by_rows(proj_sum, nothing)
        acc[...] = jnp.zeros_like(acc)

        def mixed_back(index, carry):
            item = 3 * gate_chunks + index
            slot = ready(item)
            acc[...] += mul(small[:, aligned(index * wide, wide)], ring[slot], NT)
            release(item)
            return carry

        lax.fori_loop(0, out_chunks, mixed_back, 0)
        mixed_grad[...] = acc[...].astype(low)
        loads[2].wait()
        loads[3].wait()
        for buffer in (turned_q, turned_k, turned_v):
            buffer[...] = jnp.zeros_like(buffer)

        def attend_back(head, carry):
            cols, mask = window(head, model_width)
            tile = cols.start
            q = low_buf[:, cols] * mask
            k = low_buf[:, aligned(model_width + tile, 256)] * mask
            v = low_buf[:, aligned(2 * model_width + tile, 256)]
            d_mixed = mixed_grad[:, cols] * mask
            share = prob[head]
            d_share = mul(v, d_mixed, NT)
            wide_share = share.astype(high)
            product = wide_share * d_share
            d_score = (product - wide_share * jnp.sum(product, axis=0, keepdims=True)).astype(low)
            turned_v[:, cols] = turned_v[:, cols] + mul(share, d_mixed)
            turned_k[:, cols] = turned_k[:, cols] + mul(d_score, q)
            turned_q[:, cols] = turned_q[:, cols] + mul(d_score, k, TN)
            return carry

        lax.fori_loop(0, heads, attend_back, 0, unroll=2)
        member = member_ref[...]
        for index, turned in enumerate((turned_q, turned_k)):
            cols = slice(index * model_width, (index + 1) * model_width)

            def unturn(rows, gain_sum):
                straight, crossed = turn(
                    turned[rows] * HEAD_DIM ** (-0.5),
                    cos_ref[rows],
                    first_ref[rows],
                    second_ref[rows],
                )
                d_norm = straight - crossed
                unit = high_buf[rows, cols]
                d_unit = d_norm * gain_ref[index : index + 1]
                turned[rows] = d_unit
                acc[rows] = d_unit * unit
                return gain_sum + total(d_norm * unit)

            sums[4 + index : 5 + index] = by_rows(unturn, nothing)
            level = mul_split(acc[...], member) * (1.0 / HEAD_DIM)
            rate = high_buf[:, 5 * model_width + index * PAD : 5 * model_width + (index + 1) * PAD]
            acc[...] = mul_split(rate * level, member, NT)
            dy[...] = mul_split(rate, member, NT)

            def unscale(rows, carry):
                d_raw = dy[rows] * turned[rows] - high_buf[rows, cols] * acc[rows]
                d_low = d_raw.astype(low)
                dqkv[rows, cols] = d_low
                return carry + total(d_low.astype(high))

            sums[index : index + 1] = by_rows(unscale, nothing)

        def values(rows, carry):
            d_low = turned_v[rows].astype(low)
            dqkv[rows, 2 * model_width :] = d_low
            return carry + total(d_low.astype(high))

        sums[2:3] = by_rows(values, nothing)
        send(dqkv, dqkv_out)
        acc[...] = jnp.zeros_like(acc)

        def project_back(index, carry):
            item = 3 * gate_chunks + out_chunks + index
            slot = ready(item)
            acc[...] += mul(dqkv[:, aligned(index * wide, wide)], ring[slot], NT)
            release(item)
            return carry

        lax.fori_loop(0, qkv_chunks, project_back, 0)

        def leave(rows, carry):
            scale_sum, shift_sum = carry
            x = x_ref[rows].astype(high)
            rate = rms_rate(x)
            unit = x * rate
            back = acc[rows]
            d_unit = back * (1.0 + scale1)
            grad = middle_grad[rows] + rate * (
                d_unit - unit * jnp.mean(d_unit * unit, axis=-1, keepdims=True)
            )
            mixed_grad[rows] = grad.astype(low)
            return scale_sum + total(back * unit), shift_sum + total(back)

        scale_sum, shift_sum = by_rows(leave, (nothing,) * 2)
        dmod[1:2] = scale_sum
        dmod[0:1] = shift_sum
        send(mixed_grad, dx_out)
        send(dmod, dmod_out)
        send(sums, sums_out)
        for copy in copies:
            copy.wait()


def run_backward(active, live, dy, x, weights, mod, gain, tables, member, parts, left, kept):
    model_width = x.shape[1]
    low, high = jnp.bfloat16, jnp.float32
    shapes = [
        ((LEN, model_width), low),
        ((4, model_width, LEN), low),
        ((LEN, 3 * model_width), low),
        ((LEN, model_width), low),
        ((LEN, 2 * FF), low),
        ((8, model_width), high),
        ((8, model_width), high),
    ]
    flag = pl.BlockSpec(memory_space=pltpu.SMEM)
    near = pl.BlockSpec(memory_space=pltpu.VMEM)
    far = pl.BlockSpec(memory_space=pl.ANY)
    if kept is None:
        extra, aliases = [left], {15: 1}
    else:
        extra = list(kept)
        aliases = {15 + index: index for index in range(len(extra))}
    return pl.pallas_call(
        functools.partial(backward_kernel, aliased=len(extra)),
        out_shape=[jax.ShapeDtypeStruct(shape, kind) for shape, kind in shapes],
        in_specs=[flag, flag, near, near, far] + [near] * 6 + [far] * (4 + len(extra)),
        out_specs=[far] * len(shapes),
        input_output_aliases=aliases,
        scratch_shapes=[
            pltpu.VMEM((RING, model_width, CHUNK), low),
            pltpu.VMEM((LEN, model_width), high),
            pltpu.VMEM((LEN, 3 * model_width), low),
            pltpu.VMEM((HEADS, LEN, LEN), low),
            pltpu.VMEM((LEN, 5 * model_width + 2 * PAD), high),
            pltpu.VMEM((LEN, 2 * FF), high),
            pltpu.VMEM((LEN, 2 * FF), low),
            pltpu.VMEM((LEN, 3 * model_width), low),
            pltpu.VMEM((LEN, model_width), low),
            pltpu.VMEM((model_width, LEN), low),
            pltpu.VMEM((LEN, model_width), high),
            pltpu.VMEM((LEN, model_width), high),
            pltpu.VMEM((LEN, model_width), low),
            pltpu.VMEM((LEN, model_width), high),
            pltpu.VMEM((LEN, model_width), high),
            pltpu.VMEM((LEN, model_width), high),
            pltpu.VMEM((8, model_width), high),
            pltpu.VMEM((8, model_width), high),
            pltpu.SemaphoreType.DMA((RING,)),
            pltpu.SemaphoreType.DMA((4,)),
            pltpu.SemaphoreType.DMA((10,)),
        ],
        compiler_params=pltpu.CompilerParams(vmem_limit_bytes=56 * 1024 * 1024),
        cost_estimate=pl.CostEstimate(flops=0, bytes_accessed=120_000_000, transcendentals=0),
        name="layer_backward",
    )(active, live, dy, x, weights, mod, gain, *tables, member, *parts, *extra)


def body(
    start,
    out_grad,
    extra_images,
    timesteps,
    labels,
    embed_table,
    w_qkv,
    w_out,
    w_gu,
    w_ada,
    w_down,
    small_params,
    feature_moments,
    other_moments,
    small_moment,
):
    model_width = start.shape[-1]
    section_index = lax.axis_index("section")
    shard_index = lax.axis_index("shard")
    group_index = lax.axis_index("grp")
    sections = lax.axis_size("section")
    shards = lax.axis_size("shard")
    groups = lax.axis_size("grp")
    rows = w_qkv.shape[1]
    low = jnp.bfloat16
    high = jnp.float32
    widths = (3 * model_width, model_width, 2 * FF, FF)
    starts = (0, widths[0], widths[0] + widths[1], widths[0] + widths[1] + widths[2])
    gate_up = w_gu[0].reshape(rows, 2, FF // CHUNK, CHUNK).transpose(0, 2, 1, 3)
    own = jnp.concatenate(
        [w_qkv[0], w_out[0], gate_up.reshape(rows, 2 * FF), w_down[0].T], axis=1
    ).astype(low)
    own = own.reshape(rows, sum(widths) // CHUNK, CHUNK).transpose(1, 0, 2)
    weights = gather_rows(own).reshape(own.shape[0], model_width, CHUNK)
    ada_low = w_ada[0].astype(low)
    small_all = lax.all_gather(small_params[0].astype(low), "shard", axis=0, tiled=True)
    small_all = small_all.astype(high)
    bias = small_all[None, : 4 * model_width]
    b_ada = small_all[4 * model_width : 10 * model_width]
    gain = jnp.tile(small_all[10 * model_width :].reshape(2, HEAD_DIM), (1, HEADS))
    tables = rope_tables(model_width)
    member = head_members(model_width)
    half_cond = embed_table[timesteps] + embed_table[TIMESTEPS + labels]
    cond_all = lax.all_gather(half_cond, ("section", "shard"))
    cond_all = cond_all.reshape(sections, shards * MB, half_cond.shape[1])
    cond_all = cond_all.transpose(1, 0, 2).reshape(shards * MB, model_width)
    act_all = jax.nn.silu(cond_all).astype(low)
    condition = lax.dynamic_slice_in_dim(cond_all, shard_index * MB, MB, 0)
    act_low = lax.dynamic_slice_in_dim(act_all, shard_index * MB, MB, 0)
    act_columns = lax.dynamic_slice_in_dim(act_all, shard_index * rows, rows, 1)
    partial_mod = jnp.dot(act_columns, ada_low, preferred_element_type=high)
    modulation = lax.psum_scatter(partial_mod, "shard", scatter_dimension=0, tiled=True) + b_ada
    image_count = extra_images[0] + 1
    live = [(jnp.full((1,), micro) < image_count).astype(high) for micro in range(MB)]
    here = [jnp.full((1,), section_index == index, jnp.int32) for index in range(2)]
    mods = [modulation[micro].reshape(6, model_width) for micro in range(MB)]
    fixed = (gain, tables, member)
    kept = []
    received = []
    for micro in range(MB):
        result = run_forward(
            here[0], live[micro], start[micro], weights, mods[micro], bias, *fixed, None
        )
        kept.append(result)
        received.append(passed_along(result[1], "section", 1))
    for micro in range(MB):
        kept[micro] = run_forward(
            here[1], live[micro], received[micro], weights, mods[micro], bias, *fixed, kept[micro]
        )
    section_out = jnp.stack([result[0] for result in kept])
    grads_kept = []
    returned = []
    for micro in range(MB):
        result = run_backward(
            here[1],
            live[micro],
            out_grad[micro],
            received[micro],
            weights,
            mods[micro],
            *fixed,
            kept[micro][4:],
            kept[micro][2],
            None,
        )
        grads_kept.append(result)
        returned.append(passed_along(result[0], "section", -1))
    for micro in range(MB):
        grads_kept[micro] = run_backward(
            here[0],
            live[micro],
            returned[micro],
            start[micro],
            weights,
            mods[micro],
            *fixed,
            kept[micro][4:],
            None,
            grads_kept[micro],
        )
    section_in_grad = jnp.stack([result[0] for result in grads_kept])
    lefts = [result[1].reshape(4, shards, rows, LEN) for result in grads_kept]
    rights = [
        [result[2], result[3], result[4], kept[micro][3]]
        for micro, result in enumerate(grads_kept)
    ]
    sums = sum(result[6] for result in grads_kept)
    gains = jnp.sum(sums[4:6].reshape(2, HEADS, HEAD_DIM), axis=1)
    packed = jnp.concatenate([result[5][:6] for result in grads_kept] + [sums[:4]], axis=0)
    beside = jnp.pad(gains, ((0, packed.shape[0] - 2), (0, PAD - HEAD_DIM)))
    packed = jnp.concatenate([packed, beside], axis=1).astype(low)
    images = shards * MB
    act_rows = jnp.pad(act_columns, ((0, -images % 16), (0, -rows % 128)))
    tail = jnp.pad(jnp.sum(feature_moments[0], axis=1)[None], ((0, 0), (0, CHUNK - 5)))
    reduced = reduce_grads(lefts, rights, packed, act_rows, ada_low, tail)
    sum_low = reduced[:4]
    row_squares, stats, totals, all_mod, every_act, cond_parts = reduced[4:]
    small_vector = jnp.concatenate(
        [
            totals[12:16, :model_width].reshape(-1),
            (totals[:6] + totals[6:12])[:, :model_width].reshape(-1),
            totals[:2, model_width : model_width + HEAD_DIM].reshape(-1),
        ]
    )
    small_rows = small_params.shape[1]
    small_grad = lax.dynamic_slice_in_dim(small_vector, shard_index * small_rows, small_rows, 0)
    flat_act = every_act.reshape(-1, every_act.shape[2])[:, :rows]
    grad_ada = jnp.concatenate(
        [
            lax.dot_general(flat_act, all_mod[index], TN, preferred_element_type=high)
            for index in range(6)
        ],
        axis=1,
    )
    own_part = lax.dynamic_slice_in_dim(cond_parts, shard_index * MB, MB, 1)[:, :, :rows]
    act_grad = own_part.transpose(1, 0, 2).reshape(MB, model_width)
    sigma = jax.nn.sigmoid(condition)
    cond_term = act_grad * sigma * (1.0 + condition * (1.0 - sigma))
    cond_grad = lax.dynamic_slice_in_dim(
        cond_term, section_index * half_cond.shape[1], half_cond.shape[1], 1
    )

    wide = (widths[0], widths[1], widths[2], 6 * model_width, widths[3])
    order = (0, 1, 2, 4, 3)
    row_sums = jnp.sum(row_squares, axis=-1)
    row_means = jnp.stack([row_sums[index] / width for index, width in zip(order, wide)])
    feature_new = DECAY * feature_moments[0] + (1.0 - DECAY) * row_means
    column_flat = stats[:-1].reshape(-1)
    column_all = jnp.concatenate(
        [column_flat[: starts[3]], column_flat[sum(widths) :], column_flat[starts[3] : sum(widths)]]
    )
    ends = [sum(wide[: index + 1]) for index in range(5)]
    feature_total = jnp.stack(
        [
            DECAY * stats[-1, index]
            + (1.0 - DECAY) / wide[index] * jnp.sum(column_all[ends[index] - wide[index] : ends[index]])
            for index in range(5)
        ]
    )
    other_new = DECAY * other_moments[0] + (1.0 - DECAY) * column_all / model_width
    grads = [
        sum_low[0].astype(high),
        sum_low[1].astype(high),
        sum_low[2].astype(high),
        grad_ada,
        sum_low[3].astype(high),
    ]
    masters = (w_qkv[0], w_out[0], w_gu[0], w_ada[0], w_down[0].T)
    feature_scale = lax.rsqrt(feature_new / (feature_total / model_width)[:, None])
    other_scale = lax.rsqrt(other_new)
    new_wide = []
    lower = 0
    for index in range(5):
        upper = lower + wide[index]
        new_wide.append(
            masters[index]
            - RATE
            * grads[index]
            * feature_scale[index][:, None]
            * other_scale[None, lower:upper]
        )
        lower = upper
    small_new = DECAY * small_moment[0] + (1.0 - DECAY) * (small_grad * small_grad + TINY)
    new_small = small_params[0] - RATE_SMALL * small_grad * lax.rsqrt(small_new)
    return (
        section_out[None],
        section_in_grad[None],
        cond_grad,
        grads[0][None],
        grads[1][None],
        grads[2][None],
        grads[3][None],
        grads[4].T[None],
        small_grad[None],
        new_wide[0][None],
        new_wide[1][None],
        new_wide[2][None],
        new_wide[3][None],
        new_wide[4].T[None],
        new_small[None],
        feature_new[None],
        other_new[None],
        small_new[None],
    )


def solution(mesh):
    in_specs = (
        P(("grp", "shard"), None, None),
        P(("grp", "shard"), None, None),
        P(("grp", "shard")),
        P(("grp", "shard")),
        P(("grp", "shard")),
        P(None, "section"),
        P("section", "shard", None),
        P("section", "shard", None),
        P("section", "shard", None),
        P("section", "shard", None),
        P("section", None, "shard"),
        P("section", "shard"),
        P("section", None, "shard"),
        P("section", None),
        P("section", "shard"),
    )
    out_specs = (
        P("section", ("grp", "shard"), None, None),
        P("section", ("grp", "shard"), None, None),
        P(("grp", "shard"), "section"),
        P("section", "shard", None),
        P("section", "shard", None),
        P("section", "shard", None),
        P("section", "shard", None),
        P("section", None, "shard"),
        P("section", "shard"),
        P("section", "shard", None),
        P("section", "shard", None),
        P("section", "shard", None),
        P("section", "shard", None),
        P("section", None, "shard"),
        P("section", "shard"),
        P("section", None, "shard"),
        P("section", None),
        P("section", "shard"),
    )
    return jax.shard_map(body, mesh=mesh, in_specs=in_specs, out_specs=out_specs, check_vma=False)
```

profile of v0, /device:TPU:0, one launch (start us, length us, event | category | flops | bytes accessed | tf_op | source)
XLA Modules:
  0.0 779.6 jit_solution(13675593325349410860)
XLA Ops:
  7.3 5.7 copy.81
  13.0 3.0 gather_fusion
  16.0 3.0 gather_fusion.1
  19.1 10.6 %all-gather.1 = f32[8,2,576]{2,1,0:T(2,128)S(1)} all-gather(f32[1,2,576]{2,1,0:T(2,128)S(1)} %add_bitcast_fusion), channel_id=2, replica_groups=mesh['section'=2,'grp'=4,'shard'=4] {'section','shard'}, dimensions={0}, use_global_device_ids=true | all-gather | bytes 41472 | tf_op jit(solution)/shard_map/all_gather | solution.py:1481
  29.8 5.6 convert_bitcast_fusion.3.refs_12_
  35.5 3.5 fusion.58
  39.0 3.5 convert.37
  43.3 3.6 copy.96
  46.9 4.2 reshape.369
  51.2 2.5 bitcast_convert_fusion
  56.8 3.5 pad_maximum_fusion
  63.0 11.6 %all-reduce.3 = bf16[11664]{0:T(1024)(128)(2,1)S(1)} all-reduce(bf16[11664]{0:T(1024)(128)(2,1)S(1)} %dynamic-update-slice), channel_id=1, replica_groups=mesh['section'=2,'grp'=4,'shard'=4] {'shard'}, use_global_device_ids=true, to_apply=%add.3 | all-reduce | flops 11664 | bytes 46656
  76.0 4.1 copy.95
  80.1 97.9 %gather_rows.1 = bf16[36,4,288,384]{3,2,1,0:T(8,128)(2,1)} custom-call(bf16[36,288,384]{2,1,0:T(8,128)(2,1)S(1)} %bitcast.166), custom_call_target="tpu_custom_call" | custom-call | bytes 300000000 | tf_op jit(solution)/shard_map/gather_rows/pallas_call | solution.py:203
  181.1 38.9 %layer_forward.4 = (bf16[256,1152]{1,0:T(8,128)(2,1)}, bf16[256,1152]{1,0:T(8,128)(2,1)}, bf16[4,1152,256]{2,1,0:T(8,128)(2,1)}, bf16[256,3072]{1,0:T(8,128)(2,1...) custom-call(s32[1]{0:T(128)} %bitcast.1.active, ...), custom_call_target="tpu_custom_call" | custom-call | bytes 80000000 | tf_op jit(solution)/shard_map/layer_forward/pallas_call | solution.py:1084
  220.0 1.3 collective-permute-start
  221.9 38.8 %layer_forward.6 = (bf16[256,1152]{1,0:T(8,128)(2,1)}, bf16[256,1152]{1,0:T(8,128)(2,1)}, bf16[4,1152,256]{2,1,0:T(8,128)(2,1)}, bf16[256,3072]{1,0:T(8,128)(2,1...) custom-call(s32[1]{0:T(128)} %bitcast.1.active, ...), custom_call_target="tpu_custom_call" | custom-call | bytes 80000000 | tf_op jit(solution)/shard_map/layer_forward/pallas_call | solution.py:1084
  260.7 1.3 collective-permute-start.1
  262.1 1.1 slice_bitcast_fusion.1
  264.1 2.8 layer_forward.5
  266.9 2.7 layer_backward.4
  269.5 1.3 collective-permute-start.2
  270.8 4.9 collective-permute-done.1.x_ref
  276.5 2.6 layer_forward.7
  279.2 2.7 layer_backward.6
  281.9 1.3 collective-permute-start.3
  284.6 1.4 negate_exponential_fusion
  286.0 1.1 maximum_bitcast_fusion
  287.1 51.1 %collective-permute-done.2.dy_ref = bf16[256,1152]{1,0:T(8,128)(2,1)S(1)} collective-permute-done((bf16[256,1152]{1,0:T(8,128)(2,1)}, bf16[256,1152]{1,0:T(8,128)(2,1)S(1)}, u32[]{:S(2)}, u32[]{:S(2)}) %collective-permute-start.2) | collective-permute-done | bytes 589856 | tf_op jit(solution)/shard_map/ppermute | solution.py:41
  339.1 46.6 %layer_backward.5 = (bf16[256,1152]{1,0:T(8,128)(2,1)}, bf16[4,1152,256]{2,1,0:T(8,128)(2,1)}, bf16[256,3456]{1,0:T(8,128)(2,1)}, bf16[256,1152]{1,0:T(8,128)(2,...) custom-call(s32[1]{0:T(128)} %bitcast.1.active, ...), custom_call_target="tpu_custom_call", output_to_operand_aliasing={{0}: (15, {}), {1}: (16, {}), {2}: (17, {}), {3}: (18, {}),... | custom-call | bytes 120000000 | tf_op jit(solution)/shard_map/layer_backward/pallas_call | solution.py:1402
  385.7 40.0 %collective-permute-done.3.dy_ref = bf16[256,1152]{1,0:T(8,128)(2,1)S(1)} collective-permute-done((bf16[256,1152]{1,0:T(8,128)(2,1)}, bf16[256,1152]{1,0:T(8,128)(2,1)S(1)}, u32[]{:S(2)}, u32[]{:S(2)}) %collective-permute-start.3) | collective-permute-done | bytes 589856 | tf_op jit(solution)/shard_map/ppermute | solution.py:41
  426.4 46.2 %layer_backward.7 = (bf16[256,1152]{1,0:T(8,128)(2,1)}, bf16[4,1152,256]{2,1,0:T(8,128)(2,1)}, bf16[256,3456]{1,0:T(8,128)(2,1)}, bf16[256,1152]{1,0:T(8,128)(2,...) custom-call(s32[1]{0:T(128)} %bitcast.1.active, ...), custom_call_target="tpu_custom_call", output_to_operand_aliasing={{0}: (15, {}), {1}: (16, {}), {2}: (17, {}), {3}: (18, {}),... | custom-call | bytes 120000000 | tf_op jit(solution)/shard_map/layer_backward/pallas_call | solution.py:1402
  475.0 216.4 %reduce_grads.1 = (bf16[288,3456]{1,0:T(8,128)(2,1)}, bf16[288,1152]{1,0:T(8,128)(2,1)}, bf16[288,6144]{1,0:T(8,128)(2,1)}, bf16[288,3072]{1,0:T(8,128)(2,1)}, f...) custom-call(bf16[4,4,288,256]{3,2,1,0:T(8,128)(2,1)} %bitcast.176, ...), custom_call_target="tpu_custom_call" | custom-call | bytes 600000000 | tf_op jit(solution)/shard_map/reduce_grads/pallas_call | solution.py:754
  691.4 1.4 slice_bitcast_fusion.4
  692.9 1.5 fusion.55
  694.3 1.4 slice_bitcast_fusion.6
  695.7 1.4 slice_reduce_fusion.2
  697.1 1.3 slice_reduce_fusion.4
  698.4 1.3 slice_reduce_fusion.3
  699.7 1.5 reduce_sum.74
  716.7 1.3 constant_dynamic-update-slice_fusion.5
  718.1 1.4 constant_dynamic-update-slice_fusion.4
  719.5 1.1 bitcast_dynamic-update-slice_fusion.5
  720.6 1.4 constant_dynamic-update-slice_fusion.3
  722.0 1.4 constant_dynamic-update-slice_fusion.2
  723.5 1.4 constant_dynamic-update-slice_fusion.1
  724.9 1.5 constant_dynamic-update-slice_fusion
  728.2 1.5 copy-done.31
  729.7 3.8 convert_bitcast_fusion
  733.5 2.2 convert_bitcast_fusion.1
  735.7 2.2 convert_bitcast_fusion.2
  737.9 1.1 convert_bitcast_fusion.4
  740.6 4.3 fusion.8
  744.8 1.1 bitcast_dynamic-update-slice_fusion.4
  746.6 1.1 bitcast_dynamic-update-slice_fusion.3
  747.8 1.2 bitcast_dynamic-update-slice_fusion.2
  748.9 1.1 bitcast_dynamic-update-slice_fusion.1
  750.1 1.1 bitcast_dynamic-update-slice_fusion
  752.3 4.3 fusion.2
  756.6 1.3 fusion.11
  758.6 2.7 fusion.5
  761.3 1.1 maximum_bitcast_fusion.1
  763.4 7.8 multiply_subtract_fusion
  771.2 1.4 fusion.46
  (195 shorter events, 32.6 us)
Async XLA Ops:
  7.2 172.2 %all-reduce.7.cloned.1.call-start = ((), (), s32[]{:S(2)}) async-start(), calls=%async_computation | async-start | bytes 442368
  7.2 5.8 copy-start.48
  7.3 5.7 copy-start.49
  29.8 5.6 copy-start.34
  51.2 3.2 copy-start.1
  54.4 1.3 copy-start.9
  54.4 2.4 copy-start.5
  56.8 3.5 copy-start.25
  56.8 4.6 copy-start.42
  56.8 4.6 copy-start.47
  220.0 43.2 %collective-permute-start = (bf16[256,1152]{1,0:T(8,128)(2,1)}, bf16[256,1152]{1,0:T(8,128)(2,1)S(1)}, u32[]{:S(2)}, u32[]{:S(2)}) collective-permute-start(bf16[256,1152]{1,0:T(8,128)(2,1)} %get-tuple-element.86.rest_1_), channel_id=1, source_target_pairs={{0,16},{1,17},{2,18},{3,19},{4,20},{5,21},{6,22},{7,23},{8,24},{9,... | collective-permute-start | bytes 1769480 | tf_op jit(solution)/shard_map/ppermute | solution.py:41
  221.9 40.1 %copy-start.26 = (bf16[2,256,1152]{2,1,0:T(8,128)(2,1)S(1)}, bf16[2,256,1152]{2,1,0:T(8,128)(2,1)}, u32[]{:S(2)}) copy-start(bf16[2,256,1152]{2,1,0:T(8,128)(2,1)} %param.20) | copy-start | bytes 3538948
  260.7 15.0 %collective-permute-start.1 = (bf16[256,1152]{1,0:T(8,128)(2,1)}, bf16[256,1152]{1,0:T(8,128)(2,1)S(1)}, u32[]{:S(2)}, u32[]{:S(2)}) collective-permute-start(bf16[256,1152]{1,0:T(8,128)(2,1)} %get-tuple-element.95.rest_1_), channel_id=1, source_target_pairs={{0,16},{1,17},{2,18},{3,19},{4,20},{5,21},{6,22},{7,23},{8,24},{9,... | collective-permute-start | bytes 1769480 | tf_op jit(solution)/shard_map/ppermute | solution.py:41
  263.2 0.8 copy-start.23
  269.5 68.7 %collective-permute-start.2 = (bf16[256,1152]{1,0:T(8,128)(2,1)}, bf16[256,1152]{1,0:T(8,128)(2,1)S(1)}, u32[]{:S(2)}, u32[]{:S(2)}) collective-permute-start(bf16[256,1152]{1,0:T(8,128)(2,1)} %get-tuple-element.109.rest_0_), channel_id=1, source_target_pairs={{16,0},{17,1},{18,2},{19,3},{20,4},{21,5},{22,6},{23,7},{24,8},{25... | collective-permute-start | bytes 1769480 | tf_op jit(solution)/shard_map/ppermute | solution.py:41
  275.7 0.8 copy-start.22
  279.1 4.7 copy-start.38
  279.1 5.4 copy-start.43
  279.2 6.8 copy-start.20
  279.2 6.8 copy-start.21
  281.9 143.7 %collective-permute-start.3 = (bf16[256,1152]{1,0:T(8,128)(2,1)}, bf16[256,1152]{1,0:T(8,128)(2,1)S(1)}, u32[]{:S(2)}, u32[]{:S(2)}) collective-permute-start(bf16[256,1152]{1,0:T(8,128)(2,1)} %get-tuple-element.122.rest_0_), channel_id=1, source_target_pairs={{16,0},{17,1},{18,2},{19,3},{20,4},{21,5},{22,6},{23,7},{24,8},{25... | collective-permute-start | bytes 1769480 | tf_op jit(solution)/shard_map/ppermute | solution.py:41
  338.2 0.8 copy-start.28
  425.6 0.8 copy-start.29
  426.4 46.2 %copy-start.32 = (f32[8,1152]{1,0:T(8,128)S(1)}, f32[8,1152]{1,0:T(8,128)}, u32[]{:S(2)}) copy-start(f32[8,1152]{1,0:T(8,128)} %get-tuple-element.142) | copy-start | bytes 110596
  426.4 47.2 %copy-start.36 = (f32[8,1152]{1,0:T(8,128)S(1)}, f32[8,1152]{1,0:T(8,128)}, u32[]{:S(2)}) copy-start(f32[8,1152]{1,0:T(8,128)} %get-tuple-element.140) | copy-start | bytes 110596
  475.0 227.1 %copy-start.37 = (f32[1,20736]{1,0:T(1,128)S(1)}, f32[1,20736]{1,0:T(1,128)}, u32[]{:S(2)}) copy-start(f32[1,20736]{1,0:T(1,128)} %param.32) | copy-start | bytes 248836
  691.4 26.6 %copy-start.24 = (bf16[4,16,384]{2,1,0:T(8,128)(2,1)S(1)}, bf16[4,16,384]{2,1,0:T(8,128)(2,1)}, u32[]{:S(2)}) copy-start(bf16[4,16,384]{2,1,0:T(8,128)(2,1)} %get-tuple-element.148) | copy-start | bytes 147460
  691.4 26.6 %copy-start.27 = (bf16[6,64,1152]{2,1,0:T(8,128)(2,1)S(1)}, bf16[6,64,1152]{2,1,0:T(8,128)(2,1)}, u32[]{:S(2)}) copy-start(bf16[6,64,1152]{2,1,0:T(8,128)(2,1)} %get-tuple-element.149) | copy-start | bytes 2654212
  703.0 2.4 copy-start.30
  723.5 6.2 copy-start.3
  726.4 3.3 copy-start.31
  729.7 3.8 copy-start.6
  733.5 2.2 copy-start.8
  735.7 2.2 copy-start.16
  735.7 4.9 copy-start.2
  740.5 4.3 copy-start.11
  740.5 7.2 copy-start.14
  740.6 8.4 %copy-start.15 = (f32[288,1152]{1,0:T(8,128)S(1)}, f32[288,1152]{1,0:T(8,128)}, u32[]{:S(2)}) copy-start(f32[288,1152]{1,0:T(8,128)} %get-tuple-element.200) | copy-start | bytes 3981316
  740.6 10.7 %copy-start.35 = (f32[6144]{0:T(1024)S(1)}, f32[6144]{0:T(1024)}, u32[]{:S(2)}) copy-start(f32[6144]{0:T(1024)} %slice.272) | copy-start | bytes 73732
  744.8 1.8 copy-start.13
  744.8 6.4 slice-start.2
  746.6 3.5 copy-start.12
  747.8 3.5 slice-start.3
  747.8 4.5 copy-start.4
  747.8 4.5 copy-start.45
  752.3 4.3 copy-start.10
  752.3 4.3 copy-start.17
  752.3 4.3 copy-start.39
  752.3 4.3 copy-start.46
  752.3 5.6 copy-start
  752.3 5.6 slice-start.4
  752.3 5.6 copy-start.44
  756.6 2.0 copy-start.7
  756.6 5.8 slice-start
  758.6 2.7 copy-start.18
  758.6 2.7 copy-start.19
  758.6 4.8 slice-start.1
  758.6 4.8 copy-start.33
  763.4 7.8 %copy-start.40 = (f32[2,1152]{1,0:T(2,128)S(1)}, f32[2,1152]{1,0:T(2,128)}, u32[]{:S(2)}) copy-start(f32[2,1152]{1,0:T(2,128)} %negate_exponential_fusion) | copy-start | bytes 27652
  763.4 7.8 %copy-start.41 = (f32[2,1152]{1,0:T(2,128)S(1)}, f32[2,1152]{1,0:T(2,128)}, u32[]{:S(2)}) copy-start(f32[2,1152]{1,0:T(2,128)} %reshape.376) | copy-start | bytes 27652
Sparse Core Ops, SparseCore 0:
  39.1 31.9 all-reduce.6
where the time goes:
time: 789 us; the launch traced here: 780 us
  Pallas kernels  496 us (63%)
  waiting for transfers between devices  96 us (12%)
  other arithmetic  63.5 us (8%)
  local copies, waits for them, and re-layouts  61.8 us (8%)
  between operations  23.4 us (3%)
  blocking collectives  22.2 us (3%)
  matrix products  12 us (2%)
    pallas_call x1, Pallas kernels, reduce_grads(): pl.pallas_call(functools.partial(reduce_kernel, shards, groups, firsts, p...  216 us
    pallas_call x4, Pallas kernels, run_backward(): pl.pallas_call(functools.partial(backward_kernel, aliased=len(extra)), ou...  98.2 us
    pallas_call x1, Pallas kernels, gather_rows(): pl.pallas_call(functools.partial(gather_kernel, chips), out_shape=jax.Sha...  97.9 us
    ppermute x4, waiting for transfers between devices, passed_along(): return lax.ppermute(block, axis, route)  96 us
    pallas_call x4, Pallas kernels, run_forward(): pl.pallas_call(functools.partial(forward_kernel, aliased=len(kept)), out_...  83.1 us
    unnamed x122, local copies, waits for them, and re-layouts  25.1 us
  transfers between devices with their start and end apart: 5, of which 3 were waited for; matrix products, arithmetic and copies ran while one was open for 4% of the time, Pallas kernels for 25%

commit v1 on v0

--- a/solution.py
+++ b/solution.py
@@ -33,6 +33,8 @@
 NT = (((1,), (1,)), ((), ()))
 TN = (((0,), (0,)), ((), ()))
 PAD = 128
+IN_SLOTS = 5
+OUT_SLOTS = 4
 
 
 def passed_along(block, axis, distance):
@@ -72,152 +74,359 @@
     return lax.axis_index("section"), lax.axis_index("grp"), lax.axis_index("shard")
 
 
-def gather_kernel(chips, own_ref, all_ref, here_sem, sib_sem, x_sem, z_sem, f_sem):
+def gather_kernel(
+    shards,
+    bounds,
+    cond_in,
+    small_in,
+    qkv_ref,
+    out_ref,
+    gu_ref,
+    down_ref,
+    ada_ref,
+    all_ref,
+    ada_low,
+    acts_ref,
+    mod_ref,
+    small_ref,
+    own,
+    stage,
+    ada_wide,
+    cond,
+    act,
+    part,
+    part_in,
+    chip_out,
+    chip_in,
+    load_sem,
+    ada_sem,
+    here_sem,
+    sib_sem,
+    x_sem,
+    z_sem,
+    f_sem,
+    cond_sem,
+    small_sem,
+    part_sem,
+):
     sec, grp, me = place()
+    chips = shards // 2
     core = me % 2
     chip = me // 2
     half = grp % 2
-    count = own_ref.shape[0] // 2
+    rows = own.shape[1]
+    count = own.shape[0] // 2
+    low, high = jnp.bfloat16, jnp.float32
     sibling = (sec, grp, me ^ 1)
     across = (sec, grp ^ 1, me)
+    opposite = (1 - sec, grp, me)
+
+    def chip_peer(k):
+        return (sec, grp, 2 * (chip ^ k) + core)
 
     barrier = pltpu.get_barrier_semaphore()
     pl.semaphore_signal(barrier, inc=1, device_id=sibling, device_id_type=MESH)
     pl.semaphore_signal(barrier, inc=1, device_id=across, device_id_type=MESH)
+    pl.semaphore_signal(barrier, inc=1, device_id=opposite, device_id_type=MESH)
     for k in range(1, chips):
-        pl.semaphore_signal(
-            barrier, inc=1, device_id=(sec, grp, 2 * (chip ^ k) + core), device_id_type=MESH
-        )
-    pl.semaphore_wait(barrier, chips + 1)
-
-    def chip_copy(k, step):
-        piece = 2 * step + half
+        pl.semaphore_signal(barrier, inc=1, device_id=chip_peer(k), device_id_type=MESH)
+    ada_load = pltpu.make_async_copy(ada_ref, ada_wide, ada_sem)
+    ada_load.start()
+
+    def load(step, side, start):
+        piece = 2 * step + side
+        slot = (step % 2) * 2 + side
+        target = stage.at[slot]
+        if not start:
+            pltpu.make_async_copy(
+                qkv_ref.at[:, pl.ds(0, CHUNK)], target, load_sem.at[slot]
+            ).wait()
+            return
+        sources = (qkv_ref, out_ref, gu_ref, down_ref)
+        for index, source in enumerate(sources):
+            local = piece - bounds[index]
+            if index == 2:
+                pairs = source.shape[1] // CHUNK // 2
+                local = local // 2 + pairs * (local % 2)
+
+            @pl.when((piece >= bounds[index]) & (piece < bounds[index + 1]))
+            def _():
+                begin = pl.multiple_of(local * CHUNK, CHUNK)
+                pltpu.make_async_copy(
+                    source.at[:, pl.ds(begin, CHUNK)], target, load_sem.at[slot]
+                ).start()
+
+    for side in range(2):
+        load(0, side, True)
+    pl.semaphore_wait(barrier, chips + 2)
+
+    def remote(source, target, sems, device):
         return pltpu.make_async_remote_copy(
-            src_ref=own_ref.at[piece],
-            dst_ref=all_ref.at[piece, me],
-            send_sem=x_sem.at[0, k - 1, step],
-            recv_sem=x_sem.at[1, k - 1, step],
-            device_id=(sec, grp, 2 * (chip ^ k) + core),
+            src_ref=source,
+            dst_ref=target,
+            send_sem=sems[0],
+            recv_sem=sems[1],
+            device_id=device,
             device_id_type=MESH,
         )
 
-    def chip_arrival(k, step):
+    def pair(sems, *index):
+        return sems.at[(0,) + index], sems.at[(1,) + index]
+
+    def chip_copy(k, step, owner):
         piece = 2 * step + half
-        owner = 2 * (chip ^ k) + core
-        return pltpu.make_async_remote_copy(
-            src_ref=own_ref.at[piece],
-            dst_ref=all_ref.at[piece, owner],
-            send_sem=x_sem.at[0, k - 1, step],
-            recv_sem=x_sem.at[1, k - 1, step],
-            device_id=(sec, grp, owner),
-            device_id_type=MESH,
+        return remote(
+            own.at[piece], all_ref.at[piece, owner], pair(x_sem, k - 1, step), chip_peer(k)
         )
 
-    def onward(k, step, side, sems, row, target):
-        owner = 2 * (chip ^ k) + core
+    def onward(k, step, side, sems, row, target, by_core):
+        owner = 2 * (chip ^ k) + by_core
         region = all_ref.at[2 * step + side, owner]
-        return pltpu.make_async_remote_copy(
-            src_ref=region,
-            dst_ref=region,
-            send_sem=sems.at[0, row, step],
-            recv_sem=sems.at[1, row, step],
-            device_id=target,
-            device_id_type=MESH,
+        return remote(region, region, pair(sems, row, step), target)
+
+    def beside(step, owner):
+        both = pl.ds(2 * step, 2)
+        return remote(own.at[both], all_ref.at[both, owner], pair(sib_sem, step), sibling)
+
+    def here(step):
+        both = pl.ds(2 * step, 2)
+        return pltpu.make_async_copy(own.at[both], all_ref.at[both, me], here_sem.at[step])
+
+    def cond_across():
+        region = cond.at[me, sec]
+        return remote(region, region, pair(cond_sem, 0), opposite)
+
+    def cond_from_across():
+        region = cond.at[me, 1 - sec]
+        return remote(region, region, pair(cond_sem, 0), opposite)
+
+    def cond_beside(owner):
+        return remote(cond.at[owner], cond.at[owner], pair(cond_sem, 1), sibling)
+
+    def cond_chip(k, owner):
+        region = cond.at[pl.ds(2 * owner, 2)]
+        return remote(region, region, pair(cond_sem, 1 + k), chip_peer(k))
+
+    def small_beside(owner):
+        return remote(small_ref.at[owner], small_ref.at[owner], pair(small_sem, 0), sibling)
+
+    def small_chip(k, owner):
+        region = small_ref.at[pl.ds(2 * owner, 2)]
+        return remote(region, region, pair(small_sem, k), chip_peer(k))
+
+    def part_beside(which_core):
+        return remote(part.at[which_core], part_in, pair(part_sem, 0), sibling)
+
+    def part_chip(k):
+        return remote(
+            chip_out.at[k - 1], chip_in.at[k - 1], pair(part_sem, k), chip_peer(k)
         )
 
-    def from_sibling(k, step, side, row):
-        owner = 2 * (chip ^ k) + 1 - core
-        region = all_ref.at[2 * step + side, owner]
-        return pltpu.make_async_remote_copy(
-            src_ref=region,
-            dst_ref=region,
-            send_sem=f_sem.at[0, row, step],
-            recv_sem=f_sem.at[1, row, step],
-            device_id=sibling,
-            device_id_type=MESH,
-        )
-
-    def beside(step):
-        pair = pl.ds(2 * step, 2)
-        return pltpu.make_async_remote_copy(
-            src_ref=own_ref.at[pair],
-            dst_ref=all_ref.at[pair, me],
-            send_sem=sib_sem.at[0, step],
-            recv_sem=sib_sem.at[1, step],
-            device_id=sibling,
-            device_id_type=MESH,
-        )
-
-    def start_chip(step):
-        for k in range(1, chips):
-            chip_copy(k, step).start()
-
-    for step in range(AHEAD):
-        start_chip(step)
-    here = pltpu.make_async_copy(own_ref, all_ref.at[:, me], here_sem)
-    here.start()
+    cond[me, sec] = cond_in[...]
+    cond_across().start()
+    small_ref[me] = small_in[...]
+    small_beside(me).start()
+    half_width = cond_in.shape[1]
+    ada_chunks = ada_low.shape[1] // CHUNK
+    model_width = act.shape[1]
+    thirds = 3
+
+    def modulate(step):
+        @pl.when(step == 1)
+        def _():
+            cond_from_across().wait_recv()
+            cond_beside(me).start()
+            small_beside(me ^ 1).wait_recv()
+            for k in range(1, chips):
+                small_chip(k, chip).start()
+
+        @pl.when(step == 2)
+        def _():
+            cond_beside(me ^ 1).wait_recv()
+            for k in range(1, chips):
+                cond_chip(k, chip).start()
+
+        @pl.when(step == 4)
+        def _():
+            for k in range(1, chips):
+                cond_chip(k, chip ^ k).wait_recv()
+                small_chip(k, chip ^ k).wait_recv()
+            act[...] = jnp.zeros_like(act)
+            width = model_width // 2
+            for owner in range(shards):
+                for section in range(2):
+                    value = cond[owner, section, :MB, :width]
+                    act[owner * MB : (owner + 1) * MB, section * width : (section + 1) * width] = (
+                        value * (1.0 / (1.0 + jnp.exp(-value)))
+                    )
+            shape = (model_width, acts_ref.shape[1])
+            column = lax.broadcasted_iota(jnp.int32, shape, 1)
+            wanted = (lax.broadcasted_iota(jnp.int32, shape, 0) == column + me * rows) & (
+                column < rows
+            )
+            acts_ref[...] = mul(
+                act[...].astype(low), wanted.astype(high).astype(low)
+            ).astype(low)
+            part[...] = jnp.zeros_like(part)
+            ada_load.wait()
+
+        for group in range(ada_chunks // thirds):
+
+            @pl.when(step == 5 + group)
+            def _():
+                for index in range(thirds):
+                    begin = (group * thirds + index) * CHUNK
+                    cols = slice(begin, begin + CHUNK)
+                    narrow = ada_wide[:, cols].astype(low)
+                    ada_low[:, cols] = narrow
+                    product = mul(acts_ref[:, :rows], narrow)
+                    for owner in range(shards):
+                        first = owner // 2 * MB
+                        part[owner % 2, first : first + MB, cols] = product[
+                            owner * MB : (owner + 1) * MB
+                        ]
+
+        ready = 5 + ada_chunks // thirds
+
+        @pl.when(step == ready)
+        def _():
+            part_beside(1 - core).start()
+
+        @pl.when(step == ready + 1)
+        def _():
+            part_beside(core).wait_recv()
+            part_in[...] = part_in[...] + part[core]
+            for k in range(1, chips):
+                for image in range(MB):
+                    line = pl.ds((chip ^ k) * MB + image, 1)
+                    chip_out[k - 1, image : image + 1] = part_in[line, :]
+                part_chip(k).start()
+
+        @pl.when(step == ready + 3)
+        def _():
+            for k in range(1, chips):
+                part_chip(k).wait_recv()
+            for image in range(MB):
+                value = part_in[pl.ds(chip * MB + image, 1), :]
+                for k in range(1, chips):
+                    value = value + chip_in[k - 1, image : image + 1]
+                mod_ref[image : image + 1] = value
 
     def relay(step, carry):
         @pl.when(step < count)
         def _():
+            @pl.when(step + 1 < count)
+            def _():
+                for side in range(2):
+                    load(step + 1, side, True)
+
+            for side in range(2):
+                load(step, side, False)
+                own[2 * step + side] = stage[(step % 2) * 2 + side].astype(low)
             for k in range(1, chips):
-                chip_arrival(k, step).wait_recv()
-                onward(k, step, half, z_sem, k - 1, across).start()
-                onward(k, step, half, f_sem, 2 * (k - 1), sibling).start()
-                chip_copy(k, step).wait_send()
-            beside(step).start()
-
-        @pl.when(step + AHEAD < count)
-        def _():
-            start_chip(step + AHEAD)
-
-        @pl.when(step >= LAG)
+                chip_copy(k, step, me).start()
+            here(step).start()
+            beside(step, me).start()
+
+        came = step - AHEAD
+
+        @pl.when((came >= 0) & (came < count))
         def _():
             for k in range(1, chips):
-                onward(k, step - LAG, 1 - half, z_sem, k - 1, across).wait_recv()
-                onward(k, step - LAG, 1 - half, f_sem, 2 * (k - 1) + 1, sibling).start()
-                onward(k, step - LAG, half, z_sem, k - 1, across).wait_send()
-
+                chip_copy(k, came, 2 * (chip ^ k) + core).wait_recv()
+                onward(k, came, half, z_sem, k - 1, across, core).start()
+                onward(k, came, half, f_sem, 2 * (k - 1), sibling, core).start()
+                chip_copy(k, came, me).wait_send()
+
+        passed = step - AHEAD - LAG
+
+        @pl.when(passed >= 0)
+        def _():
+            for k in range(1, chips):
+                onward(k, passed, 1 - half, z_sem, k - 1, across, core).wait_recv()
+                onward(k, passed, 1 - half, f_sem, 2 * (k - 1) + 1, sibling, core).start()
+                onward(k, passed, half, z_sem, k - 1, across, core).wait_send()
+
+        modulate(step)
         return carry
 
-    lax.fori_loop(0, count + LAG, relay, 0)
+    lax.fori_loop(0, count + AHEAD + LAG, relay, 0)
 
     def finish(step, carry):
         for k in range(1, chips):
-            onward(k, step, half, f_sem, 2 * (k - 1), sibling).wait_send()
-            onward(k, step, 1 - half, f_sem, 2 * (k - 1) + 1, sibling).wait_send()
-            from_sibling(k, step, half, 2 * (k - 1)).wait_recv()
-            from_sibling(k, step, 1 - half, 2 * (k - 1) + 1).wait_recv()
-        beside(step).wait()
+            for side, row in ((half, 2 * (k - 1)), (1 - half, 2 * (k - 1) + 1)):
+                onward(k, step, side, f_sem, row, sibling, core).wait_send()
+                onward(k, step, side, f_sem, row, sibling, 1 - core).wait_recv()
+        beside(step, me).wait_send()
+        beside(step, me ^ 1).wait_recv()
+        here(step).wait()
         return carry
 
     lax.fori_loop(0, count, finish, 0)
-    here.wait()
-
-
-def gather_rows(own):
+    cond_across().wait_send()
+    cond_beside(me).wait_send()
+    small_beside(me).wait_send()
+    part_beside(1 - core).wait_send()
+    for k in range(1, chips):
+        cond_chip(k, chip).wait_send()
+        small_chip(k, chip).wait_send()
+        part_chip(k).wait_send()
+
+
+def gather_rows(cond, small, w_qkv, w_out, w_gu, w_down, w_ada):
     shards = lax.axis_size("shard")
     chips = shards // 2
-    chunks, rows, width = own.shape
+    rows = w_qkv.shape[0]
+    model_width = rows * shards
+    widths = [matrix.shape[1] for matrix in (w_qkv, w_out, w_gu, w_down)]
+    chunks = sum(widths) // CHUNK
+    bounds = [sum(widths[:index]) // CHUNK for index in range(5)]
     count = chunks // 2
+    low, high = jnp.bfloat16, jnp.float32
+    images = shards * MB
+    act_shape = (images + -images % 16, rows + -rows % 128)
+    side = chips * MB + -(chips * MB) % 8
+    ada_width = w_ada.shape[1]
+    near = pl.BlockSpec(memory_space=pltpu.VMEM)
+    far = pl.BlockSpec(memory_space=pl.ANY)
     return pl.pallas_call(
-        functools.partial(gather_kernel, chips),
-        out_shape=jax.ShapeDtypeStruct((chunks, shards, rows, width), own.dtype),
-        in_specs=[pl.BlockSpec(memory_space=pltpu.VMEM)],
-        out_specs=pl.BlockSpec(memory_space=pl.ANY),
+        functools.partial(gather_kernel, shards, bounds),
+        out_shape=[
+            jax.ShapeDtypeStruct((chunks, shards, rows, CHUNK), low),
+            jax.ShapeDtypeStruct((rows, ada_width), low),
+            jax.ShapeDtypeStruct(act_shape, low),
+            jax.ShapeDtypeStruct((MB, ada_width), high),
+            jax.ShapeDtypeStruct((shards,) + small.shape, high),
+        ],
+        in_specs=[near, near] + [far] * 5,
+        out_specs=[far] + [near] * 4,
         scratch_shapes=[
+            pltpu.VMEM((chunks, rows, CHUNK), low),
+            pltpu.VMEM((4, rows, CHUNK), high),
+            pltpu.VMEM((rows, ada_width), high),
+            pltpu.VMEM((shards, 2) + cond.shape, high),
+            pltpu.VMEM((act_shape[0], model_width), high),
+            pltpu.VMEM((2, side, ada_width), high),
+            pltpu.VMEM((side, ada_width), high),
+            pltpu.VMEM((chips - 1, 8, ada_width), high),
+            pltpu.VMEM((chips - 1, 8, ada_width), high),
+            pltpu.SemaphoreType.DMA((4,)),
             pltpu.SemaphoreType.DMA,
+            pltpu.SemaphoreType.DMA((count,)),
             pltpu.SemaphoreType.DMA((2, count)),
             pltpu.SemaphoreType.DMA((2, chips - 1, count)),
             pltpu.SemaphoreType.DMA((2, chips - 1, count)),
             pltpu.SemaphoreType.DMA((2, 2 * (chips - 1), count)),
+            pltpu.SemaphoreType.DMA((2, chips + 1)),
+            pltpu.SemaphoreType.DMA((2, chips)),
+            pltpu.SemaphoreType.DMA((2, chips)),
         ],
         compiler_params=pltpu.CompilerParams(
-            collective_id=0, has_side_effects=True, vmem_limit_bytes=32 * 1024 * 1024
+            collective_id=0, has_side_effects=True, vmem_limit_bytes=60 * 1024 * 1024
         ),
         cost_estimate=pl.CostEstimate(flops=0, bytes_accessed=300_000_000, transcendentals=0),
         name="gather_rows",
-    )(own)
+    )(cond, small, w_qkv, w_out, w_gu, w_down, w_ada)
 
 
 def reduce_kernel(shards, groups, firsts, pieces, *refs):
@@ -797,7 +1006,7 @@
             pltpu.SemaphoreType.DMA((2, chips)),
         ],
         compiler_params=pltpu.CompilerParams(
-            collective_id=1, has_side_effects=True, vmem_limit_bytes=56 * 1024 * 1024
+            collective_id=1, has_side_effects=True, vmem_limit_bytes=60 * 1024 * 1024
         ),
         cost_estimate=pl.CostEstimate(flops=0, bytes_accessed=600_000_000, transcendentals=0),
         name="reduce_grads",
@@ -1103,7 +1312,7 @@
             pltpu.SemaphoreType.DMA((RING,)),
             pltpu.SemaphoreType.DMA((10,)),
         ],
-        compiler_params=pltpu.CompilerParams(vmem_limit_bytes=56 * 1024 * 1024),
+        compiler_params=pltpu.CompilerParams(vmem_limit_bytes=60 * 1024 * 1024),
         cost_estimate=pl.CostEstimate(flops=0, bytes_accessed=80_000_000, transcendentals=0),
         name="layer_forward",
     )(active, live, x, weights, mod, bias, gain, *tables, member, *kept)
@@ -1428,10 +1637,187 @@
             pltpu.SemaphoreType.DMA((4,)),
             pltpu.SemaphoreType.DMA((10,)),
         ],
-        compiler_params=pltpu.CompilerParams(vmem_limit_bytes=56 * 1024 * 1024),
+        compiler_params=pltpu.CompilerParams(vmem_limit_bytes=60 * 1024 * 1024),
         cost_estimate=pl.CostEstimate(flops=0, bytes_accessed=120_000_000, transcendentals=0),
         name="layer_backward",
     )(active, live, dy, x, weights, mod, gain, *tables, member, *parts, *extra)
+
+
+def update_kernel(firsts, kinds, *refs):
+    count = len(kinds)
+    lows = [kind for kind in kinds if kind != "ada"]
+    sums, refs = refs[: len(lows)], refs[len(lows) :]
+    olds, refs = refs[:count], refs[count:]
+    rowsq_ref, stats_ref, other_ref, feature_ref, mods_ref, acts_ref = refs[:6]
+    grads, refs = refs[6 : 6 + count], refs[6 + count :]
+    news, refs = refs[:count], refs[count:]
+    (
+        other_out,
+        feature_out,
+        low_buf,
+        old_buf,
+        grad_buf,
+        new_buf,
+        scales,
+        in_sem,
+        out_sem,
+    ) = refs
+    high = jnp.float32
+    rows = rowsq_ref.shape[1]
+    total = other_ref.shape[0]
+    model_width = mods_ref.shape[2]
+    bounds = list(firsts) + [total]
+    source = {}
+    line = 0
+    for index, kind in enumerate(kinds):
+        if kind != "ada":
+            source[index] = line
+            line += bounds[index + 1] - bounds[index]
+    source[kinds.index("ada")] = line
+    statistic = {index: lows.index(kind) for index, kind in enumerate(kinds) if kind != "ada"}
+    statistic[kinds.index("ada")] = len(lows)
+
+    def cols(item, index):
+        return pl.ds(pl.multiple_of((item - firsts[index]) * CHUNK, CHUNK), CHUNK)
+
+    def loads(item, index):
+        slot = item % IN_SLOTS
+        copies = [(olds[index].at[:, cols(item, index)], old_buf.at[slot])]
+        if kinds[index] != "ada":
+            copies.append(
+                (sums[lows.index(kinds[index])].at[:, cols(item, index)], low_buf.at[slot])
+            )
+        return [
+            pltpu.make_async_copy(start, end, in_sem.at[slot, number])
+            for number, (start, end) in enumerate(copies)
+        ]
+
+    def stores(item, index):
+        slot = item % OUT_SLOTS
+        copies = (
+            (grad_buf.at[slot], grads[index].at[:, cols(item, index)]),
+            (new_buf.at[slot], news[index].at[:, cols(item, index)]),
+        )
+        return [
+            pltpu.make_async_copy(start, end, out_sem.at[slot, number])
+            for number, (start, end) in enumerate(copies)
+        ]
+
+    def each(item, work):
+        for index in range(count):
+
+            @pl.when((item >= bounds[index]) & (item < bounds[index + 1]))
+            def _():
+                work(index)
+
+    def begin_loads(item):
+        def work(index):
+            for copy in loads(item, index):
+                copy.start()
+
+        each(item, work)
+
+    def end_stores(item):
+        def work(index):
+            for copy in stores(item, index):
+                copy.wait()
+
+        each(item, work)
+
+    for item in range(IN_SLOTS - 1):
+        begin_loads(item)
+
+    for index in range(count):
+        width = (bounds[index + 1] - bounds[index]) * CHUNK
+        row_sum = jnp.sum(rowsq_ref[statistic[index]], axis=1, keepdims=True)
+        feature = DECAY * feature_ref[:, index : index + 1] + (1.0 - DECAY) / width * row_sum
+        feature_out[:, index : index + 1] = feature
+        lines = stats_ref[source[index] : source[index] + bounds[index + 1] - bounds[index]]
+        squares = jnp.sum(jnp.sum(lines, axis=0, keepdims=True), axis=1, keepdims=True)
+        last = stats_ref.shape[0] - 1
+        mean = (
+            DECAY * stats_ref[last : last + 1, index : index + 1]
+            + (1.0 - DECAY) / width * squares
+        ) / model_width
+        scales[index] = lax.rsqrt(feature / mean) * RATE
+        other_out[bounds[index] : bounds[index + 1]] = (
+            DECAY * other_ref[bounds[index] : bounds[index + 1]]
+            + (1.0 - DECAY) / model_width * lines
+        )
+
+    def step(item, carry):
+        @pl.when(item + IN_SLOTS - 1 < total)
+        def _():
+            begin_loads(item + IN_SLOTS - 1)
+
+        @pl.when(item >= OUT_SLOTS)
+        def _():
+            end_stores(item - OUT_SLOTS)
+
+        place_in = item % IN_SLOTS
+        place_out = item % OUT_SLOTS
+        columns = lax.rsqrt(other_out[pl.ds(item, 1), :])
+
+        def work(index):
+            for copy in loads(item, index):
+                copy.wait()
+            if kinds[index] == "ada":
+                local = item - firsts[index]
+                split = model_width // CHUNK
+                start = pl.multiple_of((local % split) * CHUNK, CHUNK)
+                mod = mods_ref[local // split, :, pl.ds(start, CHUNK)]
+                gradient = mul(acts_ref[...], mod, TN)[:rows]
+            else:
+                gradient = low_buf[place_in].astype(high)
+            delta = gradient * scales[index] * columns
+            grad_buf[place_out] = gradient
+            new_buf[place_out] = old_buf[place_in] - delta
+            for copy in stores(item, index):
+                copy.start()
+
+        each(item, work)
+        return carry
+
+    lax.fori_loop(0, total, step, 0)
+
+    def drain(offset, carry):
+        end_stores(total - OUT_SLOTS + offset)
+        return carry
+
+    lax.fori_loop(0, OUT_SLOTS, drain, 0)
+
+
+def update_matrices(sums, olds, kinds, row_squares, stats, other, feature, mods, acts):
+    high = jnp.float32
+    rows = olds[0].shape[0]
+    widths = [old.shape[1] for old in olds]
+    firsts = [sum(widths[:index]) // CHUNK for index in range(len(widths))]
+    near = pl.BlockSpec(memory_space=pltpu.VMEM)
+    far = pl.BlockSpec(memory_space=pl.ANY)
+    shapes = [jax.ShapeDtypeStruct(old.shape, high) for old in olds]
+    return pl.pallas_call(
+        functools.partial(update_kernel, firsts, kinds),
+        out_shape=shapes
+        + shapes
+        + [
+            jax.ShapeDtypeStruct(other.shape, high),
+            jax.ShapeDtypeStruct(feature.shape, high),
+        ],
+        in_specs=[far] * (len(sums) + len(olds)) + [near] * 6,
+        out_specs=[far] * (2 * len(olds)) + [near] * 2,
+        scratch_shapes=[
+            pltpu.VMEM((IN_SLOTS, rows, CHUNK), jnp.bfloat16),
+            pltpu.VMEM((IN_SLOTS, rows, CHUNK), high),
+            pltpu.VMEM((OUT_SLOTS, rows, CHUNK), high),
+            pltpu.VMEM((OUT_SLOTS, rows, CHUNK), high),
+            pltpu.VMEM((len(olds), rows, 1), high),
+            pltpu.SemaphoreType.DMA((IN_SLOTS, 2)),
+            pltpu.SemaphoreType.DMA((OUT_SLOTS, 2)),
+        ],
+        compiler_params=pltpu.CompilerParams(vmem_limit_bytes=60 * 1024 * 1024),
+        cost_estimate=pl.CostEstimate(flops=0, bytes_accessed=90_000_000, transcendentals=0),
+        name="update_matrices",
+    )(*sums, *olds, row_squares, stats, other, feature, mods, acts)
 
 
 def body(
@@ -1454,39 +1840,29 @@
     model_width = start.shape[-1]
     section_index = lax.axis_index("section")
     shard_index = lax.axis_index("shard")
-    group_index = lax.axis_index("grp")
-    sections = lax.axis_size("section")
     shards = lax.axis_size("shard")
-    groups = lax.axis_size("grp")
     rows = w_qkv.shape[1]
     low = jnp.bfloat16
     high = jnp.float32
     widths = (3 * model_width, model_width, 2 * FF, FF)
     starts = (0, widths[0], widths[0] + widths[1], widths[0] + widths[1] + widths[2])
-    gate_up = w_gu[0].reshape(rows, 2, FF // CHUNK, CHUNK).transpose(0, 2, 1, 3)
-    own = jnp.concatenate(
-        [w_qkv[0], w_out[0], gate_up.reshape(rows, 2 * FF), w_down[0].T], axis=1
-    ).astype(low)
-    own = own.reshape(rows, sum(widths) // CHUNK, CHUNK).transpose(1, 0, 2)
-    weights = gather_rows(own).reshape(own.shape[0], model_width, CHUNK)
-    ada_low = w_ada[0].astype(low)
-    small_all = lax.all_gather(small_params[0].astype(low), "shard", axis=0, tiled=True)
-    small_all = small_all.astype(high)
+    entries = lax.broadcasted_iota(jnp.int32, (MB, embed_table.shape[0]), 1)
+    chosen = (entries == timesteps[:, None]) | (entries == TIMESTEPS + labels[:, None])
+    half_cond = jnp.dot(chosen.astype(high), embed_table, precision=lax.Precision.HIGHEST)
+    cond_block = jnp.pad(half_cond, ((0, 8 - MB), (0, -half_cond.shape[1] % 128)))
+    small_rows = small_params.shape[1]
+    small_block = jnp.pad(small_params[0], (0, -small_rows % 1024)).reshape(8, -1)
+    weights, ada_low, act_rows, modulation, small_blocks = gather_rows(
+        cond_block, small_block, w_qkv[0], w_out[0], w_gu[0], w_down[0].T, w_ada[0]
+    )
+    weights = weights.reshape(weights.shape[0], model_width, CHUNK)
+    small_all = small_blocks.reshape(shards, -1)[:, :small_rows].reshape(-1)
+    small_all = small_all.astype(low).astype(high)
     bias = small_all[None, : 4 * model_width]
-    b_ada = small_all[4 * model_width : 10 * model_width]
+    modulation = modulation + small_all[4 * model_width : 10 * model_width]
     gain = jnp.tile(small_all[10 * model_width :].reshape(2, HEAD_DIM), (1, HEADS))
     tables = rope_tables(model_width)
     member = head_members(model_width)
-    half_cond = embed_table[timesteps] + embed_table[TIMESTEPS + labels]
-    cond_all = lax.all_gather(half_cond, ("section", "shard"))
-    cond_all = cond_all.reshape(sections, shards * MB, half_cond.shape[1])
-    cond_all = cond_all.transpose(1, 0, 2).reshape(shards * MB, model_width)
-    act_all = jax.nn.silu(cond_all).astype(low)
-    condition = lax.dynamic_slice_in_dim(cond_all, shard_index * MB, MB, 0)
-    act_low = lax.dynamic_slice_in_dim(act_all, shard_index * MB, MB, 0)
-    act_columns = lax.dynamic_slice_in_dim(act_all, shard_index * rows, rows, 1)
-    partial_mod = jnp.dot(act_columns, ada_low, preferred_element_type=high)
-    modulation = lax.psum_scatter(partial_mod, "shard", scatter_dimension=0, tiled=True) + b_ada
     image_count = extra_images[0] + 1
     live = [(jnp.full((1,), micro) < image_count).astype(high) for micro in range(MB)]
     here = [jnp.full((1,), section_index == index, jnp.int32) for index in range(2)]
@@ -1546,8 +1922,6 @@
     packed = jnp.concatenate([result[5][:6] for result in grads_kept] + [sums[:4]], axis=0)
     beside = jnp.pad(gains, ((0, packed.shape[0] - 2), (0, PAD - HEAD_DIM)))
     packed = jnp.concatenate([packed, beside], axis=1).astype(low)
-    images = shards * MB
-    act_rows = jnp.pad(act_columns, ((0, -images % 16), (0, -rows % 128)))
     tail = jnp.pad(jnp.sum(feature_moments[0], axis=1)[None], ((0, 0), (0, CHUNK - 5)))
     reduced = reduce_grads(lefts, rights, packed, act_rows, ada_low, tail)
     sum_low = reduced[:4]
@@ -1559,81 +1933,39 @@
             totals[:2, model_width : model_width + HEAD_DIM].reshape(-1),
         ]
     )
-    small_rows = small_params.shape[1]
     small_grad = lax.dynamic_slice_in_dim(small_vector, shard_index * small_rows, small_rows, 0)
-    flat_act = every_act.reshape(-1, every_act.shape[2])[:, :rows]
-    grad_ada = jnp.concatenate(
-        [
-            lax.dot_general(flat_act, all_mod[index], TN, preferred_element_type=high)
-            for index in range(6)
-        ],
-        axis=1,
-    )
+    half = half_cond.shape[1]
     own_part = lax.dynamic_slice_in_dim(cond_parts, shard_index * MB, MB, 1)[:, :, :rows]
     act_grad = own_part.transpose(1, 0, 2).reshape(MB, model_width)
-    sigma = jax.nn.sigmoid(condition)
-    cond_term = act_grad * sigma * (1.0 + condition * (1.0 - sigma))
-    cond_grad = lax.dynamic_slice_in_dim(
-        cond_term, section_index * half_cond.shape[1], half_cond.shape[1], 1
+    act_grad = lax.dynamic_slice_in_dim(act_grad, section_index * half, half, 1)
+    sigma = jax.nn.sigmoid(half_cond)
+    cond_grad = act_grad * sigma * (1.0 + half_cond * (1.0 - sigma))
+    kinds = ("qkv", "out", "gu", "ada", "down")
+    lines = other_moments.shape[1] // CHUNK
+    updated = update_matrices(
+        sum_low,
+        (w_qkv[0], w_out[0], w_gu[0], w_ada[0], w_down[0].T),
+        kinds,
+        row_squares,
+        stats,
+        other_moments.reshape(lines, CHUNK),
+        feature_moments[0].T,
+        all_mod,
+        every_act.reshape(-1, every_act.shape[2]),
     )
-
-    wide = (widths[0], widths[1], widths[2], 6 * model_width, widths[3])
-    order = (0, 1, 2, 4, 3)
-    row_sums = jnp.sum(row_squares, axis=-1)
-    row_means = jnp.stack([row_sums[index] / width for index, width in zip(order, wide)])
-    feature_new = DECAY * feature_moments[0] + (1.0 - DECAY) * row_means
-    column_flat = stats[:-1].reshape(-1)
-    column_all = jnp.concatenate(
-        [column_flat[: starts[3]], column_flat[sum(widths) :], column_flat[starts[3] : sum(widths)]]
-    )
-    ends = [sum(wide[: index + 1]) for index in range(5)]
-    feature_total = jnp.stack(
-        [
-            DECAY * stats[-1, index]
-            + (1.0 - DECAY) / wide[index] * jnp.sum(column_all[ends[index] - wide[index] : ends[index]])
-            for index in range(5)
-        ]
-    )
-    other_new = DECAY * other_moments[0] + (1.0 - DECAY) * column_all / model_width
-    grads = [
-        sum_low[0].astype(high),
-        sum_low[1].astype(high),
-        sum_low[2].astype(high),
-        grad_ada,
-        sum_low[3].astype(high),
-    ]
-    masters = (w_qkv[0], w_out[0], w_gu[0], w_ada[0], w_down[0].T)
-    feature_scale = lax.rsqrt(feature_new / (feature_total / model_width)[:, None])
-    other_scale = lax.rsqrt(other_new)
-    new_wide = []
-    lower = 0
-    for index in range(5):
-        upper = lower + wide[index]
-        new_wide.append(
-            masters[index]
-            - RATE
-            * grads[index]
-            * feature_scale[index][:, None]
-            * other_scale[None, lower:upper]
-        )
-        lower = upper
+    grads = [*updated[:4], updated[4].T]
+    new_wide = [*updated[5:9], updated[9].T]
+    other_new = updated[10].reshape(-1)
+    feature_new = updated[11].T
     small_new = DECAY * small_moment[0] + (1.0 - DECAY) * (small_grad * small_grad + TINY)
     new_small = small_params[0] - RATE_SMALL * small_grad * lax.rsqrt(small_new)
     return (
         section_out[None],
         section_in_grad[None],
         cond_grad,
-        grads[0][None],
-        grads[1][None],
-        grads[2][None],
-        grads[3][None],
-        grads[4].T[None],
+        *[grad[None] for grad in grads],
         small_grad[None],
-        new_wide[0][None],
-        new_wide[1][None],
-        new_wide[2][None],
-        new_wide[3][None],
-        new_wide[4].T[None],
+        *[new[None] for new in new_wide],
         new_small[None],
         feature_new[None],
         other_new[None],

time: 789 us -> 686 us (0.87)
  other arithmetic: 63.5 us -> 6.49 us
  Pallas kernels: 496 us -> 540 us
  local copies, waits for them, and re-layouts: 61.8 us -> 21.9 us
  blocking collectives: 22.2 us -> 0 us
  between operations: 23.4 us -> 1.85 us
    pallas_call x1 -> x2, Pallas kernels: 97.9 us -> 142 us  [the longest x1 112 us: gather_rows(): pl.pallas_call(functools.partial(gather_kernel, shards, bounds), out_shap...]
    broadcast_in_dim x9 -> x0, other arithmetic: 23 us -> none  [the longest x1 4.26 us: body(): new_wide[2][None]]
    unnamed x122 -> x34, local copies, waits for them, and re-layouts: 25.1 us -> 8.15 us
    unnamed x1 -> x0, blocking collectives: 11.6 us -> none
    all_gather x1 -> x0, blocking collectives: 10.6 us -> none  [body(): cond_all = lax.all_gather(half_cond, ('section', 'shard'))]
  transfers between devices with their start and end apart: 5 -> 4, of which waited for: 3 -> 3; matrix products, arithmetic and copies ran while one was open for 4% -> 1% of each run, Pallas kernels for 25% -> 14%
where the time goes in v1:
time: 686 us; the launch traced here: 677 us
  Pallas kernels  540 us (79%)
  waiting for transfers between devices  97.1 us (14%)
  local copies, waits for them, and re-layouts  21.9 us (3%)
    pallas_call x1, Pallas kernels, reduce_grads(): pl.pallas_call(functools.partial(reduce_kernel, shards, groups, firsts, p...  216 us
    pallas_call x1, Pallas kernels, gather_rows(): pl.pallas_call(functools.partial(gather_kernel, shards, bounds), out_shap...  112 us
    pallas_call x4, Pallas kernels, run_backward(): pl.pallas_call(functools.partial(backward_kernel, aliased=len(extra)), ou...  98.8 us
    ppermute x4, waiting for transfers between devices, passed_along(): return lax.ppermute(block, axis, route)  97.1 us
    pallas_call x4, Pallas kernels, run_forward(): pl.pallas_call(functools.partial(forward_kernel, aliased=len(kept)), out_...  82.8 us
    pallas_call x1, Pallas kernels, update_matrices(): pl.pallas_call(functools.partial(update_kernel, firsts, kinds), out_shape...  29.8 us
  transfers between devices with their start and end apart: 4, of which 3 were waited for; matrix products, arithmetic and copies ran while one was open for 1% of the time, Pallas kernels for 14%

profile of v1, /device:TPU:0, one launch (start us, length us, event | category | flops | bytes accessed | tf_op | source)
XLA Modules:
  0.0 677.1 jit_solution(16323030138657564787)
XLA Ops:
  0.7 0.7 reduce.1
  1.4 0.6 reshape.117.small_in
  2.0 0.7 broadcast_add_fusion.1
  2.7 4.6 fusion.2
  7.2 0.6 pad.17.cond_in
  7.9 112.5 %gather_rows.1 = (bf16[36,4,288,384]{3,2,1,0:T(8,128)(2,1)}, bf16[288,6912]{1,0:T(8,128)(2,1)}, bf16[16,384]{1,0:T(8,128)(2,1)}, f32[2,6912]{1,0:T(2,128)}, f32[4,8,384]{2,1,0:T(8,128)}) custom-call(f32[8,640]{1,0:T(8,128)} %pad.17.cond_in, f32[8,384]{1,0:T(8,128)} %reshape.117.small_in, f32[288,3456]{1,0:T(8,128)} %bitcast.77, f32[288,1152]{1,0:T(8,128)} %bitcast.81, ...), custom_call_target="tpu_custom_call" | custom-call | bytes 300000000 | tf_op jit(solution)/shard_map/gather_rows/pallas_call | solution.py:392
  120.4 0.8 copy.75
  121.2 0.1 reshape.131
  121.3 0.1 convert_element_type.50
  121.5 0.8 broadcast_add_fusion
  122.3 0.1 slice_reduce_fusion.1
  122.5 0.6 reshape_squeeze.6.mod_ref
  123.1 0.7 tile.15.gain_ref
  123.8 0.6 broadcast_in_dim.71.bias_ref
  125.1 1.1 slice_bitcast_fusion.3
  126.2 38.7 %layer_forward.4 = (bf16[256,1152]{1,0:T(8,128)(2,1)}, bf16[256,1152]{1,0:T(8,128)(2,1)}, bf16[4,1152,256]{2,1,0:T(8,128)(2,1)}, bf16[256,3072]{1,0:T(8,128)(2,1...) custom-call(s32[1]{0:T(128)} %bitcast.1.active, ...), custom_call_target="tpu_custom_call" | custom-call | bytes 80000000 | tf_op jit(solution)/shard_map/layer_forward/pallas_call | solution.py:1293
  164.9 1.3 collective-permute-start
  166.2 0.6 reshape_squeeze.7.mod_ref
  166.8 39.3 %layer_forward.6 = (bf16[256,1152]{1,0:T(8,128)(2,1)}, bf16[256,1152]{1,0:T(8,128)(2,1)}, bf16[4,1152,256]{2,1,0:T(8,128)(2,1)}, bf16[256,3072]{1,0:T(8,128)(2,1...) custom-call(s32[1]{0:T(128)} %bitcast.1.active, ...), custom_call_target="tpu_custom_call" | custom-call | bytes 80000000 | tf_op jit(solution)/shard_map/layer_forward/pallas_call | solution.py:1293
  206.1 1.3 collective-permute-start.1
  207.5 1.1 slice_bitcast_fusion.1
  208.6 0.8 copy-done.5
  209.4 2.4 layer_forward.5
  211.9 2.8 layer_backward.4
  214.7 1.3 collective-permute-start.2
  216.0 5.1 collective-permute-done.1.x_ref
  221.1 0.8 copy-done.4
  221.9 2.4 layer_forward.7
  224.4 0.0 copy-start.13
  224.4 0.0 copy-start.14
  224.4 0.0 copy-start.12
  224.4 2.9 layer_backward.6
  227.3 1.3 collective-permute-start.3
  228.6 0.1 reduce_sum.19
  228.7 0.8 copy.73
  229.5 0.6 pad.20.refs_13_
  230.2 0.2 reduce.4
  230.4 0.6 reshape.124.refs_11_
  231.0 51.9 %collective-permute-done.2.dy_ref = bf16[256,1152]{1,0:T(8,128)(2,1)S(1)} collective-permute-done((bf16[256,1152]{1,0:T(8,128)(2,1)}, bf16[256,1152]{1,0:T(8,128)(2,1)S(1)}, u32[]{:S(2)}, u32[]{:S(2)}) %collective-permute-start.2) | collective-permute-done | bytes 589856 | tf_op jit(solution)/shard_map/ppermute | solution.py:43
  282.9 0.8 copy-done.8
  283.7 46.4 %layer_backward.5 = (bf16[256,1152]{1,0:T(8,128)(2,1)}, bf16[4,1152,256]{2,1,0:T(8,128)(2,1)}, bf16[256,3456]{1,0:T(8,128)(2,1)}, bf16[256,1152]{1,0:T(8,128)(2,...) custom-call(s32[1]{0:T(128)} %bitcast.1.active, ...), custom_call_target="tpu_custom_call", output_to_operand_aliasing={{0}: (15, {}), {1}: (16, {}), {2}: (17, {}), {3}: (18, {}),... | custom-call | bytes 120000000 | tf_op jit(solution)/shard_map/layer_backward/pallas_call | solution.py:1611
  330.1 40.1 %collective-permute-done.3.dy_ref = bf16[256,1152]{1,0:T(8,128)(2,1)S(1)} collective-permute-done((bf16[256,1152]{1,0:T(8,128)(2,1)}, bf16[256,1152]{1,0:T(8,128)(2,1)S(1)}, u32[]{:S(2)}, u32[]{:S(2)}) %collective-permute-start.3) | collective-permute-done | bytes 589856 | tf_op jit(solution)/shard_map/ppermute | solution.py:43
  370.2 0.8 copy-done.9
  371.1 46.7 %layer_backward.7 = (bf16[256,1152]{1,0:T(8,128)(2,1)}, bf16[4,1152,256]{2,1,0:T(8,128)(2,1)}, bf16[256,3456]{1,0:T(8,128)(2,1)}, bf16[256,1152]{1,0:T(8,128)(2,...) custom-call(s32[1]{0:T(128)} %bitcast.1.active, ...), custom_call_target="tpu_custom_call", output_to_operand_aliasing={{0}: (15, {}), {1}: (16, {}), {2}: (17, {}), {3}: (18, {}),... | custom-call | bytes 120000000 | tf_op jit(solution)/shard_map/layer_backward/pallas_call | solution.py:1611
  417.7 0.8 add.59
  418.5 0.1 reshape.122
  418.7 0.8 slice.115
  419.4 0.6 fusion.1.refs_10_
  420.1 216.1 %reduce_grads.1 = (bf16[288,3456]{1,0:T(8,128)(2,1)}, bf16[288,1152]{1,0:T(8,128)(2,1)}, bf16[288,6144]{1,0:T(8,128)(2,1)}, bf16[288,3072]{1,0:T(8,128)(2,1)}, f...) custom-call(bf16[4,4,288,256]{3,2,1,0:T(8,128)(2,1)} %bitcast.72, ...), custom_call_target="tpu_custom_call" | custom-call | bytes 600000000 | tf_op jit(solution)/shard_map/reduce_grads/pallas_call | solution.py:963
  636.2 1.0 fusion.14
  637.2 0.8 slice.82
  637.9 0.7 slice.86
  638.7 0.1 reshape.128
  638.7 0.1 add_multiply_fusion
  638.9 0.6 broadcast_in_dim.80
  639.5 0.6 broadcast_in_dim.86
  640.1 0.6 broadcast_in_dim.88
  640.7 29.8 %update_matrices.1 = (f32[288,3456]{1,0:T(8,128)}, f32[288,1152]{1,0:T(8,128)}, f32[288,6144]{1,0:T(8,128)}, f32[288,6912]{1,0:T(8,128)}, f32[288,3072]{1,0:T(8,...) custom-call(bf16[288,3456]{1,0:T(8,128)(2,1)} %get-tuple-element.167, ...), custom_call_target="tpu_custom_call" | custom-call | bytes 90000000 | tf_op jit(solution)/shard_map/update_matrices/pallas_call | solution.py:1798
  670.5 1.6 copy.76
  672.1 1.6 copy.74
  673.7 0.8 dynamic-slice_bitcast_fusion
  674.5 0.1 reshape.123
  674.6 0.7 add_multiply_fusion.1
  675.3 1.7 maximum_bitcast_fusion
  (40 shorter events, 0.2 us)
Async XLA Ops:
  7.9 117.2 %copy-start.6 = (bf16[2,256,1152]{2,1,0:T(8,128)(2,1)S(1)}, bf16[2,256,1152]{2,1,0:T(8,128)(2,1)}, u32[]{:S(2)}) copy-start(bf16[2,256,1152]{2,1,0:T(8,128)(2,1)} %param.19) | copy-start | bytes 3538948
  164.9 43.7 %collective-permute-start = (bf16[256,1152]{1,0:T(8,128)(2,1)}, bf16[256,1152]{1,0:T(8,128)(2,1)S(1)}, u32[]{:S(2)}, u32[]{:S(2)}) collective-permute-start(bf16[256,1152]{1,0:T(8,128)(2,1)} %get-tuple-element.106.rest_1_), channel_id=1, source_target_pairs={{0,16},{1,17},{2,18},{3,19},{4,20},{5,21},{6,22},{7,23},{8,24},{9,... | collective-permute-start | bytes 1769480 | tf_op jit(solution)/shard_map/ppermute | solution.py:43
  166.8 40.6 %copy-start.7 = (bf16[2,256,1152]{2,1,0:T(8,128)(2,1)S(1)}, bf16[2,256,1152]{2,1,0:T(8,128)(2,1)}, u32[]{:S(2)}) copy-start(bf16[2,256,1152]{2,1,0:T(8,128)(2,1)} %param.20) | copy-start | bytes 3538948
  206.1 15.0 %collective-permute-start.1 = (bf16[256,1152]{1,0:T(8,128)(2,1)}, bf16[256,1152]{1,0:T(8,128)(2,1)S(1)}, u32[]{:S(2)}, u32[]{:S(2)}) collective-permute-start(bf16[256,1152]{1,0:T(8,128)(2,1)} %get-tuple-element.115.rest_1_), channel_id=1, source_target_pairs={{0,16},{1,17},{2,18},{3,19},{4,20},{5,21},{6,22},{7,23},{8,24},{9,... | collective-permute-start | bytes 1769480 | tf_op jit(solution)/shard_map/ppermute | solution.py:43
  208.6 0.8 copy-start.5
  214.7 68.2 %collective-permute-start.2 = (bf16[256,1152]{1,0:T(8,128)(2,1)}, bf16[256,1152]{1,0:T(8,128)(2,1)S(1)}, u32[]{:S(2)}, u32[]{:S(2)}) collective-permute-start(bf16[256,1152]{1,0:T(8,128)(2,1)} %get-tuple-element.129.rest_0_), channel_id=1, source_target_pairs={{16,0},{17,1},{18,2},{19,3},{20,4},{21,5},{22,6},{23,7},{24,8},{25... | collective-permute-start | bytes 1769480 | tf_op jit(solution)/shard_map/ppermute | solution.py:43
  221.1 0.8 copy-start.4
  224.4 4.2 copy-start.13
  224.4 5.7 copy-start.14
  224.4 5.7 copy-start.12
  227.3 142.9 %collective-permute-start.3 = (bf16[256,1152]{1,0:T(8,128)(2,1)}, bf16[256,1152]{1,0:T(8,128)(2,1)S(1)}, u32[]{:S(2)}, u32[]{:S(2)}) collective-permute-start(bf16[256,1152]{1,0:T(8,128)(2,1)} %get-tuple-element.142.rest_0_), channel_id=1, source_target_pairs={{16,0},{17,1},{18,2},{19,3},{20,4},{21,5},{22,6},{23,7},{24,8},{25... | collective-permute-start | bytes 1769480 | tf_op jit(solution)/shard_map/ppermute | solution.py:43
  282.9 0.8 copy-start.8
  370.2 0.8 copy-start.9
  371.1 46.7 %copy-start.10 = (f32[8,1152]{1,0:T(8,128)S(1)}, f32[8,1152]{1,0:T(8,128)}, u32[]{:S(2)}) copy-start(f32[8,1152]{1,0:T(8,128)} %get-tuple-element.162) | copy-start | bytes 110596
  371.1 47.6 %copy-start.11 = (f32[8,1152]{1,0:T(8,128)S(1)}, f32[8,1152]{1,0:T(8,128)}, u32[]{:S(2)}) copy-start(f32[8,1152]{1,0:T(8,128)} %get-tuple-element.160) | copy-start | bytes 110596
  640.7 34.6 %copy-start = (bf16[256,1152]{1,0:T(8,128)(2,1)S(1)}, bf16[256,1152]{1,0:T(8,128)(2,1)}, u32[]{:S(2)}) copy-start(bf16[256,1152]{1,0:T(8,128)(2,1)} %get-tuple-element.136) | copy-start | bytes 1769476
  640.7 34.6 %copy-start.1 = (bf16[256,1152]{1,0:T(8,128)(2,1)S(1)}, bf16[256,1152]{1,0:T(8,128)(2,1)}, u32[]{:S(2)}) copy-start(bf16[256,1152]{1,0:T(8,128)(2,1)} %get-tuple-element.149) | copy-start | bytes 1769476
  640.7 34.6 %copy-start.2 = (bf16[256,1152]{1,0:T(8,128)(2,1)S(1)}, bf16[256,1152]{1,0:T(8,128)(2,1)}, u32[]{:S(2)}) copy-start(bf16[256,1152]{1,0:T(8,128)(2,1)} %get-tuple-element.123) | copy-start | bytes 1769476
  640.7 34.6 %copy-start.3 = (bf16[256,1152]{1,0:T(8,128)(2,1)S(1)}, bf16[256,1152]{1,0:T(8,128)(2,1)}, u32[]{:S(2)}) copy-start(bf16[256,1152]{1,0:T(8,128)(2,1)} %get-tuple-element.114) | copy-start | bytes 1769476
